TPU v7x, 32 devices: a whole 2x2x4 slice. The times are simulated.
32 devices in a mesh: seq: 8 (over z, y), batch: 4 (over x, core).
Axes of the slice: x: 2, y: 2, z: 4, core: 2. Of those that a mesh axis runs over, the one named last changes fastest.
Arguments:
- inputs: bfloat16 [8, 2048, 768], P('batch', 'seq'), may hold values from -6 to 6
- history: bfloat16 [5, 8, 2048, 768], P(None, 'batch', 'seq'), may hold values from -6 to 6
- seq_lengths: int32 [8], P('batch'), may hold values from 256 to 1024, as said below
- attn_gain: bfloat16 [768], P(('seq', 'batch')), may hold values from 0.5 to 1.5
- attn_shift: bfloat16 [768], P(('seq', 'batch')), may hold values from -3 to 3
- qkv_weight: bfloat16 [768, 2304], P(('seq', 'batch')), may hold values from -0.21875 to 0.21875
- qkv_bias: bfloat16 [2304], P(('seq', 'batch')), may hold values from -3 to 3
- out_weight: bfloat16 [768, 768], P(('seq', 'batch')), may hold values from -1.75 to 1.75
- out_bias: bfloat16 [768], P(('seq', 'batch')), may hold values from -3 to 3
- mlp_gain: bfloat16 [768], P(('seq', 'batch')), may hold values from 0.5 to 1.5
- mlp_shift: bfloat16 [768], P(('seq', 'batch')), may hold values from -3 to 3
- up_weight: bfloat16 [768, 3072], P(('seq', 'batch')), may hold values from -0.21875 to 0.21875
- up_bias: bfloat16 [3072], P(('seq', 'batch')), may hold values from -3 to 3
- down_weight: bfloat16 [3072, 768], P(('seq', 'batch')), may hold values from -0.109375 to 0.109375
- down_bias: bfloat16 [768], P(('seq', 'batch')), may hold values from -3 to 3
- mix_weights: float32 [6], replicated, may hold values from 0.2 to 1
- cotangent: bfloat16 [8, 2048, 768], P('batch', 'seq'), may hold values from -6 to 6
Outputs:
- layer_out: bfloat16 [8, 2048, 768], P('batch', 'seq')
- grad_inputs: bfloat16 [8, 2048, 768], P('batch', 'seq')
- grad_history: bfloat16 [5, 8, 2048, 768], P(None, 'batch', 'seq')
- grad_attn_gain: float32 [768], P(('seq', 'batch'))
- grad_attn_shift: float32 [768], P(('seq', 'batch'))
- grad_qkv_weight: float32 [768, 2304], P(('seq', 'batch'))
- grad_qkv_bias: float32 [2304], P(('seq', 'batch'))
- grad_out_weight: float32 [768, 768], P(('seq', 'batch'))
- grad_out_bias: float32 [768], P(('seq', 'batch'))
- grad_mlp_gain: float32 [768], P(('seq', 'batch'))
- grad_mlp_shift: float32 [768], P(('seq', 'batch'))
- grad_up_weight: float32 [768, 3072], P(('seq', 'batch'))
- grad_up_bias: float32 [3072], P(('seq', 'batch'))
- grad_down_weight: float32 [3072, 768], P(('seq', 'batch'))
- grad_down_bias: float32 [768], P(('seq', 'batch'))
- grad_mix_weights: float32 [6], replicated
Inputs may be any that keep to these rules, and one draw needn't show every extreme that they name: `seq_lengths`: each entry is 1024 or 256; both values occur in every draw.
All inputs are finite; a program needn't handle non-finite values.
Results may differ from a plain program's by a relative error of at most 0.028.
Values may be sent and summed in bfloat16 or wider, within the bound.
A program may use at most 320 MiB of HBM per device.

v0:
```python
import math

import jax
import jax.numpy as jnp
from jax import lax
from jax.sharding import PartitionSpec as P

HEADS = 12
HEAD_DIM = 64
LONG_LEN = 1024
SHORT_LEN = 256


eps = 1e-05
masked = -1e30


def block_size(row_count):
    chosen = 1
    for candidate in range(1, min(row_count, 512) + 1):
        if row_count % candidate == 0:
            chosen = candidate
    return chosen


def exact_gelu(values):
    return jax.nn.gelu(values, approximate=False)


def layer_norm(values, norm_gain, norm_shift):
    average = jnp.mean(values, axis=-1, keepdims=True)
    centred = values - average
    inverse = lax.rsqrt(jnp.mean(centred * centred, axis=-1, keepdims=True) + eps)
    normed = centred * inverse
    return (normed * norm_gain + norm_shift, normed, inverse)


def norm_back(grad_out, normed, inverse, norm_gain):
    grad_normed = grad_out * norm_gain
    mean_grad = jnp.mean(grad_normed, axis=-1, keepdims=True)
    mean_cross = jnp.mean(grad_normed * normed, axis=-1, keepdims=True)
    grad_in = inverse * (grad_normed - mean_grad - normed * mean_cross)
    return (grad_in, jnp.sum(grad_out * normed, axis=0), jnp.sum(grad_out, axis=0))


def token_layout(index, info):
    seq_len, tok_count, slice_len = info
    is_long = seq_len == LONG_LEN
    offset = index % tok_count
    device = index // tok_count
    doc_ids = jnp.where(is_long, offset // slice_len, index // SHORT_LEN).astype(jnp.int32)
    relative = jnp.where(
        is_long, device * slice_len + offset % slice_len, index % SHORT_LEN
    ).astype(jnp.int32)
    return (doc_ids, relative)


def rotary_tables(relative):
    half_dim = HEAD_DIM // 2
    frequency = jnp.exp(
        -math.log(10000.0) * (2.0 * jnp.arange(half_dim, dtype=jnp.float32) / HEAD_DIM)
    )
    angles = relative.astype(jnp.float32)[:, None] * frequency[None, :]
    return (jnp.cos(angles)[:, None, :], jnp.sin(angles)[:, None, :])


def rotate(values, cosine, sine_table):
    half_dim = values.shape[-1] // 2
    lower_half = values[..., :half_dim]
    upper_half = values[..., half_dim:]
    return jnp.concatenate(
        [
            lower_half * cosine - upper_half * sine_table,
            upper_half * cosine + lower_half * sine_table,
        ],
        axis=-1,
    )


def allowed_mask(query_places, key_places, info):
    query_docs, query_rel = token_layout(query_places, info)
    key_docs, key_rel = token_layout(key_places, info)
    return (key_docs[None, :] == query_docs[:, None]) & (key_rel[None, :] <= query_rel[:, None])


def online_block(current, query_b, key_block, value_block, query_places, key_places, info):
    running, denominator, weighted = current
    key_count = key_block.shape[0]
    allowed = allowed_mask(query_places, key_places, info)
    key_heads = key_block.reshape(key_count, HEADS, HEAD_DIM)
    scores = jnp.einsum(
        "qhd,khd->hqk", query_b, key_heads, preferred_element_type=jnp.float32
    ) * HEAD_DIM ** (-0.5)
    scores = jnp.where(allowed[None], scores, masked)
    new_max = jnp.maximum(running, jnp.max(scores, axis=-1))
    exp_scores = jnp.where(allowed[None], jnp.exp(scores - new_max[..., None]), 0.0)
    rescale = jnp.exp(running - new_max)
    denominator = denominator * rescale + jnp.sum(exp_scores, axis=-1)
    value_heads = value_block.reshape(key_count, HEADS, HEAD_DIM)
    weighted = weighted * rescale[..., None] + jnp.einsum(
        "hqk,khd->hqd",
        exp_scores.astype(jnp.bfloat16),
        value_heads,
        preferred_element_type=jnp.float32,
    )
    return (new_max, denominator, weighted)


def attend_rows(current, query_b, key_rows, value_rows, first_row, query_places, info, last_place):
    key_count = key_rows.shape[0]
    block_rows = block_size(key_count)

    def one_block(carried, block_index):
        start_place = first_row + block_index * block_rows
        key_block = lax.dynamic_slice_in_dim(key_rows, block_index * block_rows, block_rows, 0)
        value_block = lax.dynamic_slice_in_dim(value_rows, block_index * block_rows, block_rows, 0)
        key_places = start_place + jnp.arange(block_rows, dtype=jnp.int32)

        def one_compute(state_in):
            return online_block(
                state_in, query_b, key_block, value_block, query_places, key_places, info
            )

        def unchanged(state_in):
            return state_in

        return (lax.cond(start_place > last_place, unchanged, one_compute, carried), None)

    result, unused = lax.scan(
        one_block, current, jnp.arange(key_count // block_rows, dtype=jnp.int32)
    )
    return result


def block_probs(query_b, key_b, query_places, key_places, info, lse_rows):
    allowed = allowed_mask(query_places, key_places, info)
    scores = jnp.einsum(
        "qhd,khd->hqk", query_b, key_b, preferred_element_type=jnp.float32
    ) * HEAD_DIM ** (-0.5)
    return jnp.exp(jnp.where(allowed[None], scores - lse_rows[..., None], masked))


def block_dscores(probabilities, grad_b, value_b, delta_rows):
    dprobs = jnp.einsum("qhd,khd->hqk", grad_b, value_b, preferred_element_type=jnp.float32)
    return (probabilities * (dprobs - delta_rows[..., None])).astype(jnp.bfloat16)


def shards(
    inputs,
    history,
    seq_lengths,
    attn_gain,
    attn_shift,
    qkv_weight,
    qkv_bias,
    out_weight,
    out_bias,
    mlp_gain,
    mlp_shift,
    up_weight,
    up_bias,
    down_weight,
    down_bias,
    mix_weights,
    cotangent,
):
    group_count = inputs.shape[0]
    tok_count = inputs.shape[1]
    model_width = inputs.shape[2]
    seq_count = lax.axis_size("seq")
    group_rows = tok_count * seq_count
    slice_len = LONG_LEN // seq_count
    factor = HEAD_DIM ** (-0.5)
    seq_index = lax.axis_index("seq")
    first_place = seq_index * tok_count
    last_place = first_place + tok_count - 1
    places = first_place + jnp.arange(tok_count, dtype=jnp.int32)
    gathered = (
        lax.all_gather(attn_gain, ("seq", "batch"), axis=0, tiled=True),
        lax.all_gather(attn_shift, ("seq", "batch"), axis=0, tiled=True),
        lax.all_gather(qkv_weight, ("seq", "batch"), axis=0, tiled=True),
        lax.all_gather(qkv_bias, ("seq", "batch"), axis=0, tiled=True),
        lax.all_gather(out_weight, ("seq", "batch"), axis=0, tiled=True),
        lax.all_gather(out_bias, ("seq", "batch"), axis=0, tiled=True),
        lax.all_gather(mlp_gain, ("seq", "batch"), axis=0, tiled=True),
        lax.all_gather(mlp_shift, ("seq", "batch"), axis=0, tiled=True),
        lax.all_gather(up_weight, ("seq", "batch"), axis=0, tiled=True),
        lax.all_gather(up_bias, ("seq", "batch"), axis=0, tiled=True),
        lax.all_gather(down_weight, ("seq", "batch"), axis=0, tiled=True),
        lax.all_gather(down_bias, ("seq", "batch"), axis=0, tiled=True),
    )
    (
        gain_one,
        shift_one,
        qkv_full,
        qkv_vec,
        out_full,
        out_vec,
        gain_two,
        shift_two,
        up_full,
        up_vec,
        down_full,
        down_vec,
    ) = gathered
    saved = []
    block_outs = []
    for group in range(group_count):
        info = (seq_lengths[group], tok_count, slice_len)
        doc_ids, relative = token_layout(places, info)
        cosine, sine_table = rotary_tables(relative)
        residual_in = inputs[group].astype(jnp.float32)
        normed_out, normed_one, inverse_one = layer_norm(
            residual_in, gain_one.astype(jnp.float32), shift_one.astype(jnp.float32)
        )
        acts_one = normed_out.astype(jnp.bfloat16)
        projected = jnp.dot(
            acts_one, qkv_full, preferred_element_type=jnp.float32
        ) + qkv_vec.astype(jnp.float32)
        queries = rotate(
            projected[:, :model_width].reshape(tok_count, HEADS, HEAD_DIM), cosine, sine_table
        ).astype(jnp.bfloat16)
        key_flat = (
            rotate(
                projected[:, model_width : 2 * model_width].reshape(tok_count, HEADS, HEAD_DIM),
                cosine,
                sine_table,
            )
            .reshape(tok_count, model_width)
            .astype(jnp.bfloat16)
        )
        value_flat = projected[:, 2 * model_width :].astype(jnp.bfloat16)
        start_state = (
            jnp.full((HEADS, tok_count), masked, jnp.float32),
            jnp.zeros((HEADS, tok_count), jnp.float32),
            jnp.zeros((HEADS, tok_count, HEAD_DIM), jnp.float32),
        )
        key_all = None
        value_all = None
        running, denominator, weighted = attend_rows(
            start_state,
            queries,
            lax.all_gather(key_flat, "seq", axis=0, tiled=True),
            lax.all_gather(value_flat, "seq", axis=0, tiled=True),
            jnp.int32(0),
            places,
            info,
            last_place,
        )
        attended = jnp.transpose(weighted / denominator[..., None], (1, 0, 2))
        lse_rows = running + jnp.log(denominator)
        attended_b = attended.reshape(tok_count, model_width).astype(jnp.bfloat16)
        middle = (
            residual_in
            + jnp.dot(attended_b, out_full, preferred_element_type=jnp.float32)
            + out_vec.astype(jnp.float32)
        )
        normed_out_two, normed_two, inverse_two = layer_norm(
            middle, gain_two.astype(jnp.float32), shift_two.astype(jnp.float32)
        )
        acts_two = normed_out_two.astype(jnp.bfloat16)
        upward = jnp.dot(acts_two, up_full, preferred_element_type=jnp.float32) + up_vec.astype(
            jnp.float32
        )
        activated, gelu_back = jax.vjp(exact_gelu, upward)
        activated_b = activated.astype(jnp.bfloat16)
        block_out = (
            middle
            + jnp.dot(activated_b, down_full, preferred_element_type=jnp.float32)
            + down_vec.astype(jnp.float32)
        )
        block_outs.append(block_out)
        saved.append(
            (
                info,
                cosine,
                sine_table,
                normed_one,
                inverse_one,
                acts_one,
                queries,
                key_flat,
                value_flat,
                key_all,
                value_all,
                attended,
                lse_rows,
                attended_b,
                normed_two,
                inverse_two,
                acts_two,
                gelu_back,
                activated_b,
            )
        )
    block_stack = jnp.stack(block_outs, axis=0)
    earlier = history.astype(jnp.float32)
    grad_out_all = cotangent.astype(jnp.float32)
    mixed_out = (
        jnp.sum(mix_weights[:-1, None, None, None] * earlier, axis=0)
        + mix_weights[-1] * block_stack
    )
    mix_terms = jnp.concatenate(
        [
            jnp.sum(earlier * grad_out_all[None], axis=(1, 2, 3)),
            jnp.sum(block_stack * grad_out_all)[None],
        ]
    )
    grad_history = (mix_weights[:-1, None, None, None] * grad_out_all[None]).astype(jnp.bfloat16)
    back_gain_one, back_qkv, back_out, back_gain_two, back_up, back_down = (
        lax.all_gather(attn_gain, ("seq", "batch"), axis=0, tiled=True),
        lax.all_gather(qkv_weight, ("seq", "batch"), axis=0, tiled=True),
        lax.all_gather(out_weight, ("seq", "batch"), axis=0, tiled=True),
        lax.all_gather(mlp_gain, ("seq", "batch"), axis=0, tiled=True),
        lax.all_gather(up_weight, ("seq", "batch"), axis=0, tiled=True),
        lax.all_gather(down_weight, ("seq", "batch"), axis=0, tiled=True),
    )
    totals = None
    grad_input_list = []
    for group in range(group_count):
        (
            info,
            cosine,
            sine_table,
            normed_one,
            inverse_one,
            acts_one,
            queries,
            key_flat,
            value_flat,
            key_all,
            value_all,
            attended,
            lse_rows,
            attended_b,
            normed_two,
            inverse_two,
            acts_two,
            gelu_back,
            activated_b,
        ) = saved[group]
        grad_block = mix_weights[-1] * grad_out_all[group]
        down_grad_b = grad_block.astype(jnp.bfloat16)
        grad_w_down = jnp.einsum(
            "tf,td->fd", activated_b, down_grad_b, preferred_element_type=jnp.float32
        )
        grad_b_down = jnp.sum(down_grad_b.astype(jnp.float32), axis=0)
        grad_act = jnp.einsum(
            "td,fd->tf", down_grad_b, back_down, preferred_element_type=jnp.float32
        )
        up_grad_b = gelu_back(grad_act)[0].astype(jnp.bfloat16)
        grad_w_up = jnp.einsum("td,tf->df", acts_two, up_grad_b, preferred_element_type=jnp.float32)
        grad_b_up = jnp.sum(up_grad_b.astype(jnp.float32), axis=0)
        grad_acts_two = jnp.einsum(
            "tf,df->td", up_grad_b, back_up, preferred_element_type=jnp.float32
        )
        grad_middle_norm, grad_gain_two, grad_shift_two = norm_back(
            grad_acts_two, normed_two, inverse_two, back_gain_two.astype(jnp.float32)
        )
        grad_middle = grad_block + grad_middle_norm
        attn_grad_b = grad_middle.astype(jnp.bfloat16)
        grad_w_out = jnp.einsum(
            "te,td->ed", attended_b, attn_grad_b, preferred_element_type=jnp.float32
        )
        grad_b_out = jnp.sum(attn_grad_b.astype(jnp.float32), axis=0)
        grad_heads = (
            jnp.einsum("td,ed->te", attn_grad_b, back_out, preferred_element_type=jnp.float32)
            .astype(jnp.bfloat16)
            .reshape(tok_count, HEADS, HEAD_DIM)
        )
        delta_rows = jnp.transpose(jnp.sum(grad_heads.astype(jnp.float32) * attended, axis=-1))
        key_all, value_all = (
            lax.all_gather(key_flat, "seq", axis=0, tiled=True),
            lax.all_gather(value_flat, "seq", axis=0, tiled=True),
        )
        key_block_rows = block_size(group_rows)

        def query_grad_block(carried, block_index):
            start_place = block_index * key_block_rows
            key_block = lax.dynamic_slice_in_dim(key_all, start_place, key_block_rows, 0).reshape(
                key_block_rows, HEADS, HEAD_DIM
            )
            value_block = lax.dynamic_slice_in_dim(
                value_all, start_place, key_block_rows, 0
            ).reshape(key_block_rows, HEADS, HEAD_DIM)
            key_places = start_place + jnp.arange(key_block_rows, dtype=jnp.int32)

            def query_compute(summed):
                probabilities = block_probs(queries, key_block, places, key_places, info, lse_rows)
                dscores = block_dscores(probabilities, grad_heads, value_block, delta_rows)
                return (
                    summed
                    + jnp.einsum(
                        "hqk,khd->qhd", dscores, key_block, preferred_element_type=jnp.float32
                    )
                    * factor
                )

            return (
                lax.cond(start_place > last_place, lambda summed: summed, query_compute, carried),
                None,
            )

        grad_queries, unused = lax.scan(
            query_grad_block,
            jnp.zeros((tok_count, HEADS, HEAD_DIM), jnp.float32),
            jnp.arange(group_rows // key_block_rows, dtype=jnp.int32),
        )
        key_first_row = jnp.int32(0)
        key_rows = key_all
        value_rows = value_all
        inner_rows = block_size(lax.axis_size("seq") * tok_count)

        def key_grad_block(carried, block_index):
            offset = block_index * inner_rows
            start_place = key_first_row + offset
            key_block = lax.dynamic_slice_in_dim(key_rows, offset, inner_rows, 0).reshape(
                inner_rows, HEADS, HEAD_DIM
            )
            value_block = lax.dynamic_slice_in_dim(value_rows, offset, inner_rows, 0).reshape(
                inner_rows, HEADS, HEAD_DIM
            )
            key_places = start_place + jnp.arange(inner_rows, dtype=jnp.int32)

            def key_compute(unused_in):
                probabilities = block_probs(queries, key_block, places, key_places, info, lse_rows)
                dscores = block_dscores(probabilities, grad_heads, value_block, delta_rows)
                grad_keys = (
                    jnp.einsum("hqk,qhd->khd", dscores, queries, preferred_element_type=jnp.float32)
                    * factor
                )
                grad_values = jnp.einsum(
                    "hqk,qhd->khd",
                    probabilities.astype(jnp.bfloat16),
                    grad_heads,
                    preferred_element_type=jnp.float32,
                )
                return jnp.concatenate(
                    [
                        grad_keys.reshape(inner_rows, model_width),
                        grad_values.reshape(inner_rows, model_width),
                    ],
                    axis=1,
                )

            def nothing(unused_in):
                return jnp.zeros((inner_rows, 2 * model_width), jnp.float32)

            return (carried, lax.cond(start_place > last_place, nothing, key_compute, carried))

        unused_out, blocks = lax.scan(
            key_grad_block,
            jnp.int32(0),
            jnp.arange(lax.axis_size("seq") * tok_count // inner_rows, dtype=jnp.int32),
        )
        key_grads = lax.psum_scatter(
            blocks.reshape(lax.axis_size("seq") * tok_count, 2 * model_width).astype(jnp.bfloat16),
            "seq",
            scatter_dimension=0,
            tiled=True,
        ).astype(jnp.float32)
        grad_keys_own = key_grads[:, :model_width]
        grad_values_own = key_grads[:, model_width:]
        grad_q_turned = rotate(grad_queries, cosine, -sine_table).reshape(tok_count, model_width)
        grad_k_turned = rotate(
            grad_keys_own.reshape(tok_count, HEADS, HEAD_DIM), cosine, -sine_table
        ).reshape(tok_count, model_width)
        qkv_grad_b = jnp.concatenate(
            [grad_q_turned, grad_k_turned, grad_values_own], axis=1
        ).astype(jnp.bfloat16)
        grad_w_qkv = jnp.einsum(
            "td,te->de", acts_one, qkv_grad_b, preferred_element_type=jnp.float32
        )
        grad_b_qkv = jnp.sum(qkv_grad_b.astype(jnp.float32), axis=0)
        grad_acts_one = jnp.einsum(
            "te,de->td", qkv_grad_b, back_qkv, preferred_element_type=jnp.float32
        )
        grad_in_norm, grad_gain_one, grad_shift_one = norm_back(
            grad_acts_one, normed_one, inverse_one, back_gain_one.astype(jnp.float32)
        )
        grad_input_list.append((grad_middle + grad_in_norm).astype(jnp.bfloat16))
        terms = [
            grad_gain_one,
            grad_shift_one,
            grad_w_qkv,
            grad_b_qkv,
            grad_w_out,
            grad_b_out,
            grad_gain_two,
            grad_shift_two,
            grad_w_up,
            grad_b_up,
            grad_w_down,
            grad_b_down,
        ]
        if totals is None:
            totals = terms
        else:
            totals = [older + newer for older, newer in zip(totals, terms)]
    shares = (
        lax.psum_scatter(totals[0], ("seq", "batch"), scatter_dimension=0, tiled=True),
        lax.psum_scatter(totals[1], ("seq", "batch"), scatter_dimension=0, tiled=True),
        lax.psum_scatter(totals[2], ("seq", "batch"), scatter_dimension=0, tiled=True),
        lax.psum_scatter(totals[3], ("seq", "batch"), scatter_dimension=0, tiled=True),
        lax.psum_scatter(totals[4], ("seq", "batch"), scatter_dimension=0, tiled=True),
        lax.psum_scatter(totals[5], ("seq", "batch"), scatter_dimension=0, tiled=True),
        lax.psum_scatter(totals[6], ("seq", "batch"), scatter_dimension=0, tiled=True),
        lax.psum_scatter(totals[7], ("seq", "batch"), scatter_dimension=0, tiled=True),
        lax.psum_scatter(totals[8], ("seq", "batch"), scatter_dimension=0, tiled=True),
        lax.psum_scatter(totals[9], ("seq", "batch"), scatter_dimension=0, tiled=True),
        lax.psum_scatter(totals[10], ("seq", "batch"), scatter_dimension=0, tiled=True),
        lax.psum_scatter(totals[11], ("seq", "batch"), scatter_dimension=0, tiled=True),
    )
    grad_mix = lax.psum(mix_terms, ("seq", "batch"))
    grad_inputs = jnp.stack(grad_input_list, axis=0)
    return (
        mixed_out.astype(jnp.bfloat16),
        grad_inputs,
        grad_history,
        shares[0],
        shares[1],
        shares[2],
        shares[3],
        shares[4],
        shares[5],
        shares[6],
        shares[7],
        shares[8],
        shares[9],
        shares[10],
        shares[11],
        grad_mix,
    )


def solution(mesh):
    return jax.shard_map(
        shards,
        mesh=mesh,
        in_specs=(
            P("batch", "seq", None),
            P(None, "batch", "seq", None),
            P("batch"),
            P(("seq", "batch")),
            P(("seq", "batch")),
            P(("seq", "batch"), None),
            P(("seq", "batch")),
            P(("seq", "batch"), None),
            P(("seq", "batch")),
            P(("seq", "batch")),
            P(("seq", "batch")),
            P(("seq", "batch"), None),
            P(("seq", "batch")),
            P(("seq", "batch"), None),
            P(("seq", "batch")),
            P(),
            P("batch", "seq", None),
        ),
        out_specs=(
            P("batch", "seq", None),
            P("batch", "seq", None),
            P(None, "batch", "seq", None),
            P(("seq", "batch")),
            P(("seq", "batch")),
            P(("seq", "batch"), None),
            P(("seq", "batch")),
            P(("seq", "batch"), None),
            P(("seq", "batch")),
            P(("seq", "batch")),
            P(("seq", "batch")),
            P(("seq", "batch"), None),
            P(("seq", "batch")),
            P(("seq", "batch"), None),
            P(("seq", "batch")),
            P(),
        ),
        check_vma=False,
    )
```

profile of v0, /device:TPU:0, one launch (start us, length us, event | category | flops | bytes accessed | tf_op | source)
XLA Modules:
  0.0 1391.9 jit_solution(4809939453607190686)
XLA Ops:
  14.7 42.9 %all-reduce.17 = (bf16[2304]{0:T(1024)(128)(2,1)S(1)}, bf16[768]{0:T(1024)(128)(2,1)S(1)}, bf16[768]{0:T(1024)(128)(2,1)S(1)}, bf16[768]{0:T(1024)(128)(2,1)S(1)...) all-reduce(bf16[2304]{0:T(1024)(128)(2,1)S(1)} %dynamic-update-slic, ...), channel_id=1, replica_groups=mesh['seq'=8,'batch'=4] {'seq','batch'}, use_global_device_ids=true, to_apply=%add.2 | all-reduce | flops 9984 | bytes 39936
  60.5 13.3 all-gather.9.cloned.1.call-done
  106.2 32.5 %all-gather.23.cloned.1.call-done = bf16[2048,768]{1,0:T(8,128)(2,1)} async-done(((bf16[256,768]{1,0:T(8,128)(2,1)}), bf16[2048,768]{1,0:T(8,128)(2,1)}) %all-gather.23.cloned.1.call-update) | async-done | bytes 3145744 | tf_op jit(solution)/shard_map/all_gather | solution.py:244
  143.4 56.7 %all-gather.13.cloned.1.call-done = bf16[2048,768]{1,0:T(8,128)(2,1)} async-done(((bf16[256,768]{1,0:T(8,128)(2,1)}), bf16[2048,768]{1,0:T(8,128)(2,1)}) %all-gather.13.cloned.1.call-update) | async-done | bytes 3145744 | tf_op jit(solution)/shard_map/all_gather | solution.py:244
  204.8 59.4 %all-gather.21.cloned.1.call-done = bf16[2048,768]{0,1:T(8,128)(2,1)} async-done(((bf16[256,768]{0,1:T(8,128)(2,1)}), bf16[2048,768]{0,1:T(8,128)(2,1)}) %all-gather.21.cloned.1.call-update) | async-done | bytes 3145744 | tf_op jit(solution)/shard_map/all_gather | solution.py:243
  264.3 13.0 while.81
  265.6 7.7 conditional.19
  277.4 50.6 %all-gather.11.cloned.1.call-done = bf16[2048,768]{0,1:T(8,128)(2,1)} async-done(((bf16[256,768]{0,1:T(8,128)(2,1)}), bf16[2048,768]{0,1:T(8,128)(2,1)}) %all-gather.11.cloned.1.call-update) | async-done | bytes 3145744 | tf_op jit(solution)/shard_map/all_gather | solution.py:243
  328.0 14.2 %while.80 = (s32[]{:T(128)}, f32[12,256]{1,0:T(8,128)S(1)}, f32[12,256]{1,0:T(8,128)S(1)}, f32[12,256,64]{1,2,0:T(8,128)S(1)}, s32[4]{0:T(128)S(1)}, /*index=5*/...) while((s32[]{:T(128)}, f32[12,256]{1,0:T(8,128)S(1)}, ...), condition=%wide.region_8.9_spmd.clone, body=%wide.region_3.8_spmd.clone.sunk | while | flops 423930880 | bytes 26301808 | solution.py:129
  329.3 8.7 conditional.18
  343.3 39.7 %all-gather.15.cloned.1.call-done = bf16[768,768]{1,0:T(8,128)(2,1)} async-done(((bf16[24,768]{1,0:T(8,128)(2,1)}), bf16[768,768]{1,0:T(8,128)(2,1)}) %all-gather.15.cloned.1.call-update) | async-done | bytes 1179664 | tf_op jit(solution)/shard_map/all_gather | solution.py:183
  388.8 59.6 %all-gather.17.cloned.1.call-done = bf16[768,3072]{1,0:T(8,128)(2,1)} async-done(((bf16[24,3072]{1,0:T(8,128)(2,1)}), bf16[768,3072]{1,0:T(8,128)(2,1)}) %all-gather.17.cloned.1.call-update) | async-done | bytes 4718608 | tf_op jit(solution)/shard_map/all_gather | solution.py:187
  457.6 56.2 %all-gather.19.cloned.1.call-done = bf16[3072,768]{1,0:T(8,128)(2,1)} async-done(((bf16[96,768]{1,0:T(8,128)(2,1)}), bf16[3072,768]{1,0:T(8,128)(2,1)}) %all-gather.19.cloned.1.call-update) | async-done | bytes 4718608 | tf_op jit(solution)/shard_map/all_gather | solution.py:189
  513.9 12.1 convert_reduce_fusion
  531.4 10.8 convert_reduce_fusion.1
  554.7 30.4 %while.85 = (s32[]{:T(128)}, bf16[4,512,1536]{2,1,0:T(8,128)(2,1)}, s32[4]{0:T(128)S(1)}, s32[]{:T(128)}, s32[]{:T(128)}, /*index=5*/bf16[2048,768]{0,1:T(8,128)...) while((s32[]{:T(128)}, bf16[4,512,1536]{2,1,0:T(8,128)(2,1)}, ...), condition=%wide.region_45.46_spmd.clone, body=%wide.region_42.45_spmd.clone.sunk | while | flops 825398272 | bytes 36627980 | solution.py:451
  556.0 16.9 %conditional.23 = (bf16[1,512,1536]{1,2,0:T(8,128)(2,1)S(1)}) conditional(s32[]{:T(128)} %convert_element_type.508, (s32[]{:T(128)}, s32[]{:T(128)}, s32[512]{0:T(512)S(1)}, s32[]{:T(128)}, bf16[2048,768]{0,1:T(8,128)(2,1)}, /*index=5*/bf16[256,12,64]{0,2,1:T(8,128)(2,1)S(1)}, f32[12,256]{1,0:T(8,128)}, bf16[2048,768]{0,1:T(8,128)(2,1)}, ...), branch_computations={%region_43.43_spmd, %region_44.44_spmd} | conditional | flops 825398272 | bytes 30332998 | solution.py:449
  594.2 31.5 %while.83 = (s32[]{:T(128)}, bf16[4,512,1536]{2,1,0:T(8,128)(2,1)}, s32[4]{0:T(128)S(1)}, s32[]{:T(128)}, s32[]{:T(128)}, /*index=5*/bf16[2048,768]{0,1:T(8,128)...) while((s32[]{:T(128)}, bf16[4,512,1536]{2,1,0:T(8,128)(2,1)}, ...), condition=%wide.region_31.32_spmd.clone, body=%wide.region_28.31_spmd.clone.sunk | while | flops 825398272 | bytes 36627796 | solution.py:451
  595.7 18.0 %conditional.21 = (bf16[1,512,1536]{1,2,0:T(8,128)(2,1)S(1)}) conditional(s32[]{:T(128)} %convert_element_type.506, (s32[]{:T(128)}, s32[]{:T(128)}, s32[512]{0:T(512)S(1)}, s32[]{:T(128)}, bf16[2048,768]{0,1:T(8,128)(2,1)}, /*index=5*/bf16[256,12,64]{0,2,1:T(8,128)(2,1)}, f32[12,256]{1,0:T(8,128)}, bf16[2048,768]{0,1:T(8,128)(2,1)}, ...), branch_computations={%region_29.29_spmd, %region_30.30_spmd} | conditional | flops 825398272 | bytes 30332998 | solution.py:449
  653.6 19.7 %while.82 = (s32[]{:T(128)}, f32[256,12,64]{0,2,1:T(8,128)}, s32[4]{0:T(128)S(1)}, s32[]{:T(128)}, s32[]{:T(128)}, /*index=5*/bf16[2048,768]{0,1:T(8,128)(2,1)},...) while((s32[]{:T(128)}, f32[256,12,64]{0,2,1:T(8,128)}, ...), condition=%wide.region_27.28_spmd.clone, body=%wide.region_24.27_spmd.clone.sunk | while | flops 614241280 | bytes 20755800 | solution.py:404
  654.9 14.5 %conditional.20 = (f32[256,12,64]{0,2,1:T(8,128)}) conditional(s32[]{:T(128)} %convert_element_type.505, (s32[]{:T(128)}, s32[]{:T(128)}, s32[512]{0:T(512)S(1)}, s32[]{:T(128)}, bf16[2048,768]{0,1:T(8,128)(2,1)}, /*index=5*/bf16[256,12,64]{0,2,1:T(8,128)(2,1)}, f32[12,256]{1,0:T(8,128)}, bf16[2048,768]{0,1:T(8,128)(2,1)}, ...), branch_computations={%region_25.25_spmd, %region_26.26_spmd} | conditional | flops 614241280 | bytes 20752454 | solution.py:400
  662.8 6.6 fusion.67
  674.3 18.7 %while.84 = (s32[]{:T(128)}, f32[256,12,64]{0,2,1:T(8,128)}, s32[4]{0:T(128)S(1)}, s32[]{:T(128)}, s32[]{:T(128)}, /*index=5*/bf16[2048,768]{0,1:T(8,128)(2,1)},...) while((s32[]{:T(128)}, f32[256,12,64]{0,2,1:T(8,128)}, ...), condition=%wide.region_41.42_spmd.clone, body=%wide.region_38.41_spmd.clone.sunk | while | flops 614241280 | bytes 20755800 | solution.py:404
  675.5 13.4 conditional.22
  682.5 6.5 fusion.124
  693.1 59.1 %reduce-scatter.9.cloned.1.call-done = bf16[256,1536]{1,0:T(8,128)(2,1)} async-done(((bf16[2048,1536]{1,0:T(8,128)(2,1)}), bf16[256,1536]{1,0:T(8,128)(2,1)}) %reduce-scatter.9.cloned.1.call-update) | async-done | bytes 786448 | tf_op jit(solution)/shard_map/reduce_scatter | solution.py:456
  755.1 117.6 %reduce-scatter.7.cloned.1.call-done = bf16[256,1536]{1,0:T(8,128)(2,1)} async-done(((bf16[2048,1536]{1,0:T(8,128)(2,1)}), bf16[256,1536]{1,0:T(8,128)(2,1)}) %reduce-scatter.7.cloned.1.call-update) | async-done | bytes 786448 | tf_op jit(solution)/shard_map/reduce_scatter | solution.py:456
  887.8 5.9 fusion.169
  910.6 50.6 %all-reduce.16 = (f32[768]{0:T(1024)S(1)}, f32[768]{0:T(1024)S(1)}, f32[2304]{0:T(1024)S(1)}, f32[768]{0:T(1024)S(1)}, f32[768]{0:T(1024)S(1)}, /*index=5*/f32[7...) all-reduce(f32[768]{0:T(1024)} %add.889, ...), channel_id=4, replica_groups=mesh['seq'=8,'batch'=4] {'seq','batch'}, use_global_device_ids=true, to_apply=%region_51.52.clone | all-reduce | flops 9990 | bytes 79920
  976.9 142.0 %reduce-scatter.15.cloned.1.call-done = f32[24,3072]{1,0:T(8,128)} async-done(((f32[768,3072]{1,0:T(8,128)}), f32[24,3072]{1,0:T(8,128)}) %reduce-scatter.15.cloned.1.call-update) | async-done | bytes 294928 | tf_op jit(solution)/shard_map/reduce_scatter | solution.py:509
  1118.9 141.0 %reduce-scatter.17.cloned.1.call-done = f32[96,768]{1,0:T(8,128)} async-done(((f32[3072,768]{1,0:T(8,128)}), f32[96,768]{1,0:T(8,128)}) %reduce-scatter.17.cloned.1.call-update) | async-done | bytes 294928 | tf_op jit(solution)/shard_map/reduce_scatter | solution.py:511
  1259.8 125.3 %reduce-scatter.11.cloned.1.call-done = f32[24,2304]{1,0:T(8,128)} async-done(((f32[768,2304]{1,0:T(8,128)}), f32[24,2304]{1,0:T(8,128)}) %reduce-scatter.11.cloned.1.call-update) | async-done | bytes 221200 | tf_op jit(solution)/shard_map/reduce_scatter | solution.py:503
  (618 shorter events, 265.5 us)
Async XLA Ops:
  7.2 66.6 %all-gather.9.cloned.1.call-start = ((), (), s32[]{:S(2)}) async-start(), calls=%async_computation.6 | async-start | bytes 3649536 | tf_op jit(solution)/shard_map/all_gather | solution.py:181
  7.9 130.8 %all-gather.23.cloned.1.call-start = ((), (), s32[]{:S(2)}) async-start(), calls=%async_computation.13 | async-start | bytes 3538944 | tf_op jit(solution)/shard_map/all_gather | solution.py:244
  79.3 120.7 %all-gather.13.cloned.1.call-start = ((), (), s32[]{:S(2)}) async-start(), calls=%async_computation.8 | async-start | bytes 3538944 | tf_op jit(solution)/shard_map/all_gather | solution.py:244
  84.9 179.3 %all-gather.21.cloned.1.call-start = ((), (), s32[]{:S(2)}) async-start(), calls=%async_computation.12 | async-start | bytes 3538944 | tf_op jit(solution)/shard_map/all_gather | solution.py:243
  91.6 236.3 %all-gather.11.cloned.1.call-start = ((), (), s32[]{:S(2)}) async-start(), calls=%async_computation.7 | async-start | bytes 3538944 | tf_op jit(solution)/shard_map/all_gather | solution.py:243
  97.7 285.3 %all-gather.15.cloned.1.call-start = ((), (), s32[]{:S(2)}) async-start(), calls=%async_computation.9 | async-start | bytes 1216512 | tf_op jit(solution)/shard_map/all_gather | solution.py:183
  98.2 350.3 %all-gather.17.cloned.1.call-start = ((), (), s32[]{:S(2)}) async-start(), calls=%async_computation.10 | async-start | bytes 4866048 | tf_op jit(solution)/shard_map/all_gather | solution.py:187
  99.0 414.9 %all-gather.19.cloned.1.call-start = ((), (), s32[]{:S(2)}) async-start(), calls=%async_computation.11 | async-start | bytes 4866048 | tf_op jit(solution)/shard_map/all_gather | solution.py:189
  99.7 652.4 %reduce-scatter.9.cloned.1.call-start = ((), (), s32[]{:S(2)}) async-start(), calls=%async_computation.15 | async-start | bytes 7077888 | tf_op jit(solution)/shard_map/reduce_scatter | solution.py:456
  277.3 65.0 %copy-start.58 = (f32[12,256]{1,0:T(8,128)}, f32[12,256]{1,0:T(8,128)S(1)}, u32[]{:S(2)}) copy-start(f32[12,256]{1,0:T(8,128)S(1)} %get-tuple-element.1157) | copy-start | bytes 36868
  385.0 159.5 %copy-start.12 = (f32[256,768]{1,0:T(8,128)}, f32[256,768]{1,0:T(8,128)S(1)}, u32[]{:S(2)}) copy-start(f32[256,768]{1,0:T(8,128)S(1)} %get-tuple-element.1852) | copy-start | bytes 2359300
  387.1 157.5 %copy-start.89 = (f32[256]{0:T(256)}, f32[256]{0:T(256)S(1)}, u32[]{:S(2)}) copy-start(f32[256]{0:T(256)S(1)} %broadcast_multiply_fusion.10) | copy-start | bytes 3076
  388.2 156.4 %copy-start.103 = (f32[256]{0:T(256)}, f32[256]{0:T(256)S(1)}, u32[]{:S(2)}) copy-start(f32[256]{0:T(256)S(1)} %add_rsqrt_fusion) | copy-start | bytes 3076
  388.2 156.4 %copy-start.101 = (f32[256]{0:T(256)}, f32[256]{0:T(256)S(1)}, u32[]{:S(2)}) copy-start(f32[256]{0:T(256)S(1)} %add_rsqrt_fusion.2) | copy-start | bytes 3076
  388.8 65.5 %copy-start.70 = (f32[768]{0:T(1024)S(1)}, f32[768]{0:T(1024)}, u32[]{:S(2)}) copy-start(f32[768]{0:T(1024)} %convert_element_type.270) | copy-start | bytes 9220
  388.8 65.5 %copy-start.72 = (f32[768]{0:T(1024)S(1)}, f32[768]{0:T(1024)}, u32[]{:S(2)}) copy-start(f32[768]{0:T(1024)} %convert_element_type.271) | copy-start | bytes 9220
  388.8 65.5 %copy-start.92 = (f32[256]{0:T(256)S(1)}, f32[256]{0:T(256)}, u32[]{:S(2)}) copy-start(f32[256]{0:T(256)} %copy-done.91) | copy-start | bytes 3076
  388.8 65.5 %copy-start.105 = (f32[3072]{0:T(1024)S(1)}, f32[3072]{0:T(1024)}, u32[]{:S(2)}) copy-start(f32[3072]{0:T(1024)} %convert_element_type.273) | copy-start | bytes 36868
  454.3 59.5 %copy-start.46 = (bf16[256,768]{1,0:T(8,128)(2,1)S(1)}, bf16[256,768]{1,0:T(8,128)(2,1)}, u32[]{:S(2)}) copy-start(bf16[256,768]{1,0:T(8,128)(2,1)} %get-tuple-element.1805) | copy-start | bytes 1179652
  585.1 287.6 %reduce-scatter.7.cloned.1.call-start = ((), (), s32[]{:S(2)}) async-start(), calls=%async_computation.14 | async-start | bytes 7077888 | tf_op jit(solution)/shard_map/reduce_scatter | solution.py:456
  625.8 351.0 %reduce-scatter.13.cloned.1.call-start = ((), (), s32[]{:S(2)}) async-start(), calls=%async_computation.17 | async-start | bytes 2433024 | tf_op jit(solution)/shard_map/reduce_scatter | solution.py:505
  629.6 489.3 %reduce-scatter.15.cloned.1.call-start = ((), (), s32[]{:S(2)}) async-start(), calls=%async_computation.18 | async-start | bytes 9732096 | tf_op jit(solution)/shard_map/reduce_scatter | solution.py:509
  638.2 621.6 %reduce-scatter.17.cloned.1.call-start = ((), (), s32[]{:S(2)}) async-start(), calls=%async_computation.19 | async-start | bytes 9732096 | tf_op jit(solution)/shard_map/reduce_scatter | solution.py:511
  652.6 732.6 %reduce-scatter.11.cloned.1.call-start = ((), (), s32[]{:S(2)}) async-start(), calls=%async_computation.16 | async-start | bytes 7299072 | tf_op jit(solution)/shard_map/reduce_scatter | solution.py:503
  693.0 61.3 %copy-start.43 = (f32[256,12,64]{0,2,1:T(8,128)S(1)}, f32[256,12,64]{0,2,1:T(8,128)}, u32[]{:S(2)}) copy-start(f32[256,12,64]{0,2,1:T(8,128)} %get-tuple-element.1162) | copy-start | bytes 2359300
  693.0 61.3 %copy-start.77 = (f32[256,32]{0,1:T(8,128)S(1)}, f32[256,32]{0,1:T(8,128)}, u32[]{:S(2)}) copy-start(f32[256,32]{0,1:T(8,128)} %copy-done.76) | copy-start | bytes 98308
  693.0 61.3 %copy-start.79 = (f32[256,32]{0,1:T(8,128)S(1)}, f32[256,32]{0,1:T(8,128)}, u32[]{:S(2)}) copy-start(f32[256,32]{0,1:T(8,128)} %get-tuple-element.1848) | copy-start | bytes 98308
  754.7 120.4 %copy-start.75 = (f32[256,32]{0,1:T(8,128)S(1)}, f32[256,32]{0,1:T(8,128)}, u32[]{:S(2)}) copy-start(f32[256,32]{0,1:T(8,128)} %copy-done.74) | copy-start | bytes 98308
  754.7 120.4 %copy-start.78 = (f32[256,32]{0,1:T(8,128)S(1)}, f32[256,32]{0,1:T(8,128)}, u32[]{:S(2)}) copy-start(f32[256,32]{0,1:T(8,128)} %get-tuple-element.1840) | copy-start | bytes 98308
  754.9 127.2 %copy-start.32 = (bf16[256,768]{1,0:T(8,128)(2,1)}, bf16[256,768]{1,0:T(8,128)(2,1)S(1)}, u32[]{:S(2)}) copy-start(bf16[256,768]{1,0:T(8,128)(2,1)S(1)} %copy.113) | copy-start | bytes 1179652
  755.1 127.0 %copy-start.34 = (bf16[256,768]{1,0:T(8,128)(2,1)}, bf16[256,768]{1,0:T(8,128)(2,1)S(1)}, u32[]{:S(2)}) copy-start(bf16[256,768]{1,0:T(8,128)(2,1)S(1)} %copy.114) | copy-start | bytes 1179652
  906.2 62.3 %copy-start.11 = (f32[256,768]{1,0:T(8,128)S(1)}, f32[256,768]{1,0:T(8,128)}, u32[]{:S(2)}) copy-start(f32[256,768]{1,0:T(8,128)} %copy-done.9) | copy-start | bytes 2359300
  (112 other events, 635.9 us)
Sparse Core Ops, SparseCore 0:
  10.9 62.8 all-gather.8
  79.4 59.2 all-gather.22
  140.9 59.0 all-gather.12
  202.5 61.6 all-gather.20
  266.7 61.2 all-gather.10
  330.7 52.2 all-gather.14
  385.9 62.5 all-gather.16
  451.4 62.4 all-gather.18
  585.2 166.8 reduce-scatter.8
  755.6 117.0 reduce-scatter.6
  878.5 98.3 reduce-scatter.12
  984.2 134.5 reduce-scatter.14
  1125.3 134.4 reduce-scatter.16
  1266.9 118.2 reduce-scatter.10
where the time goes:
time: 1400 us; the launch traced here: 1390 us
  waiting for transfers between devices  961 us (69%)
  matrix products  138 us (10%)
  local copies, waits for them, and re-layouts  99.9 us (7%)
  blocking collectives  93.6 us (7%)
  other arithmetic  58.5 us (4%)
  loops' own time  21.9 us (2%)
  between operations  17.2 us (1%)
    reduce_scatter x2, waiting for transfers between devices, shards(): lax.psum_scatter(blocks.reshape(lax.axis_size('seq') * tok_count, 2 * mod...  177 us
    reduce_scatter x1, waiting for transfers between devices, shards(): lax.psum_scatter(totals[8], ('seq', 'batch'), scatter_dimension=0, tiled=...  142 us
    reduce_scatter x1, waiting for transfers between devices, shards(): lax.psum_scatter(totals[10], ('seq', 'batch'), scatter_dimension=0, tiled...  141 us
    reduce_scatter x1, waiting for transfers between devices, shards(): lax.psum_scatter(totals[2], ('seq', 'batch'), scatter_dimension=0, tiled=...  125 us
    all_gather x2, waiting for transfers between devices, shards(): lax.all_gather(key_flat, 'seq', axis=0, tiled=True)  110 us
    unnamed x2, blocking collectives  93.6 us
    all_gather x2, waiting for transfers between devices, shards(): lax.all_gather(value_flat, 'seq', axis=0, tiled=True)  89.2 us
    all_gather x1, waiting for transfers between devices, shards(): lax.all_gather(up_weight, ('seq', 'batch'), axis=0, tiled=True)  59.6 us
  transfers between devices with their start and end apart: 14, of which 14 were waited for; matrix products, arithmetic and copies ran while one was open for 15% of the time, Pallas kernels for 0%

commit v1 on v0

--- a/solution.py
+++ b/solution.py
@@ -1,8 +1,12 @@
+import functools
 import math
 
 import jax
 import jax.numpy as jnp
+import numpy as np
 from jax import lax
+from jax.experimental import pallas as pl
+from jax.experimental.pallas import tpu as pltpu
 from jax.sharding import PartitionSpec as P
 
 HEADS = 12
@@ -533,9 +537,9 @@
     )
 
 
-def solution(mesh):
+def placed(mesh, body):
     return jax.shard_map(
-        shards,
+        body,
         mesh=mesh,
         in_specs=(
             P("batch", "seq", None),
@@ -576,3 +580,735 @@
         ),
         check_vma=False,
     )
+
+MESH = pl.DeviceIdType.MESH
+BF, F32 = jnp.bfloat16, jnp.float32
+
+
+def where_am_i():
+    seq, batch = lax.axis_index("seq"), lax.axis_index("batch")
+    return seq // 2, seq % 2, batch // 2, batch % 2
+
+
+def dev(z, y, x, k):
+    return (z * 2 + y, x * 2 + k)
+
+
+def remote(src, dst, ssem, rsem, device):
+    return pltpu.make_async_remote_copy(src_ref=src, dst_ref=dst, send_sem=ssem, recv_sem=rsem,
+                                        device_id=device, device_id_type=MESH)
+
+
+def greet(z, y, x, k):
+    barrier = pltpu.get_barrier_semaphore()
+    mine = (z * 2 + y) * 2 + k
+    for step in range(1, 16):
+        other = lax.rem(mine + step, 16)
+        pl.semaphore_signal(barrier, inc=1, device_id=dev(other // 4, (other // 2) % 2, x, other % 2), device_id_type=MESH)
+    pl.semaphore_signal(barrier, inc=1, device_id=dev(z, y, 1 - x, k), device_id_type=MESH)
+    pl.semaphore_wait(barrier, 16)
+
+
+class Gather:
+    def __init__(self, part, send, recv, pos):
+        self.part, self.send, self.recv, self.pos = part, send, recv, pos
+        z, y, x, k = pos
+        self.c = []
+        p2 = jnp.where(k == 0, 1 - y, y), jnp.where(k == 0, x, 1 - x)
+        p3 = jnp.where(k == 0, y, 1 - y), jnp.where(k == 0, 1 - x, x)
+        d4 = 1 - y, 1 - x
+        own = (y, x)
+        zed = lambda i: part((slice(z, z + 1) if False else pl.ds(z, 1)), y, x, k)
+        allz = lambda yx: part(slice(None), yx[0], yx[1], k)
+        def cp(n, ref, device):
+            return remote(ref, ref, send.at[n], recv.at[n], device)
+        self.zs = [cp(d - 1, zed(0), dev(lax.rem(z + d, 4), y, x, k)) for d in (1, 2, 3)]
+        self.a2 = cp(3, allz(own), dev(z, *p2, k))
+        self.a3 = cp(4, allz(own), dev(z, *p3, k))
+        self.b3 = cp(5, allz(p2), dev(z, *p3, k))
+        sib = dev(z, y, x, 1 - k)
+        self.s1 = cp(6, allz(own), sib)
+        self.s2 = cp(7, allz(p2), sib)
+        self.s3 = cp(8, allz(p3), sib)
+        self.s4 = cp(9, allz(d4), sib)
+
+    def stage(self, n):
+        if n == 0:
+            for c in self.zs: c.start()
+        elif n == 1:
+            for c in self.zs: c.wait_recv()
+            self.a2.start(); self.a3.start(); self.s1.start()
+        elif n == 2:
+            self.a2.wait_recv()
+            self.b3.start(); self.s2.start()
+        elif n == 3:
+            self.a3.wait_recv()
+            self.s3.start()
+        elif n == 4:
+            self.b3.wait_recv()
+            self.s4.start()
+        elif n == 5:
+            for c in (self.s1, self.s2, self.s3, self.s4): c.wait_recv()
+            for c in self.zs + [self.a2, self.a3, self.b3, self.s1, self.s2, self.s3, self.s4]: c.wait_send()
+    STAGES = 6
+
+
+def gather_kernel(cols, qkv, out, up, down, vec, xin, cin,
+                  QKV, OUT, UP, DOWN, VEC, XM, XA, CM, CA,
+                  f_own, f_sib, block, psend, precv, lsem, gsend, grecv, asend, arecv, aarecv, fsend, frecv):
+    pos = z, y, x, k = where_am_i()
+    greet(z, y, x, k)
+    at = 0
+    tot = sum(cols)
+    offs = []
+    for n, ref in zip(cols, (qkv, out, up)):
+        half = n // 2
+        f_own[0, :, at:at + half] = ref[:, :half].astype(F32)
+        f_own[1, :, at:at + half] = ref[:, half:].astype(F32)
+        offs.append((at, half))
+        at += half
+    pre = remote(f_own.at[1 - k], f_sib, psend, precv, dev(z, y, x, 1 - k))
+    pre.start()
+    s = 2 * z + y
+    own_s = lax.rem(y + z, 2)
+    acps = []
+    for a, (src, M, A) in enumerate(((xin, XM, XA), (cin, CM, CA))):
+        for i in range(2):
+            g = 2 * k + i
+            lo = src.at[i, pl.ds(pl.multiple_of(y * 128, 128), 128)]
+            hi = src.at[i, pl.ds(pl.multiple_of((1 - y) * 128, 128), 128)]
+            for n, (ref, dst, rs, d) in enumerate((
+                (lo, M.at[s], arecv.at[a, s], (g, y, x, own_s)),
+                (hi, M.at[s], arecv.at[a, s], (g, 1 - y, x, own_s)),
+                (hi, A.at[z], aarecv.at[a, z], (g, y, x, 1 - own_s)))):
+                ss = asend.at[a, i, n]
+                me = (g == z) & (d[1] == y) & (d[3] == k)
+                cp = remote(ref, dst, ss, rs, dev(*d))
+                @pl.when(me)
+                def _():
+                    pltpu.make_async_copy(ref, dst, rs).start()
+                @pl.when(jnp.logical_not(me))
+                def _():
+                    cp.start()
+                acps.append((cp, me))
+    pre.wait_recv()
+    lcs = []
+    for i, ((at, half), W) in enumerate(zip(offs, (QKV, OUT, UP))):
+        mine = f_own[k, :, at:at + half]
+        theirs = f_sib[:, at:at + half]
+        first = jnp.where(k == 0, mine, theirs)
+        second = jnp.where(k == 0, theirs, mine)
+        block[:, at:at + half] = jnp.concatenate([first, second], axis=0).astype(BF)
+        c = pltpu.make_async_copy(block.at[:, at:at + half],
+                                  W.at[z, y, x, :, pl.ds(pl.multiple_of(k * half, 128), half)], lsem.at[i])
+        c.start(); lcs.append(c)
+    for i, (ref, W) in enumerate(((down, DOWN), (vec, VEC))):
+        c = pltpu.make_async_copy(ref, W.at[z, y, x, k], lsem.at[3 + i])
+        c.start(); lcs.append(c)
+    def colpart(W, half):
+        return lambda zz, yy, xx, kk: W.at[zz, yy, xx, :, pl.ds(pl.multiple_of(kk * half, 128), half)]
+    def rowpart(W):
+        return lambda zz, yy, xx, kk: W.at[zz, yy, xx, kk]
+    parts = [rowpart(VEC), colpart(QKV, offs[0][1]), colpart(OUT, offs[1][1]), colpart(UP, offs[2][1]), rowpart(DOWN)]
+    for c in lcs: c.wait()
+    gs = [Gather(p, gsend.at[i], grecv.at[i], pos) for i, p in enumerate(parts)]
+    fw = []
+    def tokens_forward():
+        for zz in range(4):
+            j = 2 * zz + lax.rem(zz + k, 2)
+            cp = remote(XM.at[j], XM.at[j], fsend.at[zz], frecv.at[zz], dev(z, y, x, 1 - k))
+            remote(XM.at[j], XM.at[j], fsend.at[zz], arecv.at[0, j], dev(z, y, x, 1 - k)).wait_recv()
+            cp.start(); fw.append(cp)
+        for e in range(2):
+            zz = lax.rem(1 - y + k, 2) + 2 * e
+            cp = remote(XA.at[zz], XA.at[zz], fsend.at[4 + e], frecv.at[4 + e], dev(z, y, x, 1 - k))
+            remote(XA.at[zz], XA.at[zz], fsend.at[4 + e], aarecv.at[0, zz], dev(z, y, x, 1 - k)).wait_recv()
+            cp.start(); fw.append(cp)
+    for tick in range(len(gs) + Gather.STAGES - 1):
+        for i, g in enumerate(gs):
+            n = tick - i
+            if 0 <= n < Gather.STAGES:
+                g.stage(n)
+        if tick == 2:
+            tokens_forward()
+    for zz in range(4):
+        j = 2 * zz + lax.rem(zz + k, 2)
+        remote(CM.at[j], CM.at[j], fsend.at[zz], arecv.at[1, j], dev(z, y, x, 1 - k)).wait_recv()
+    for e in range(2):
+        zz = lax.rem(1 - y + k, 2) + 2 * e
+        remote(CA.at[zz], CA.at[zz], fsend.at[4 + e], aarecv.at[1, zz], dev(z, y, x, 1 - k)).wait_recv()
+    for c in fw: c.wait()
+    for cp, me in acps:
+        @pl.when(jnp.logical_not(me))
+        def _():
+            cp.wait_send()
+    pre.wait_send()
+
+
+def gather_call(qkv, out, up, down, vec, xin, cin):
+    D = xin.shape[-1]
+    cols = (qkv.shape[1], out.shape[1], up.shape[1])
+    H = sum(cols) // 2
+    sd = jax.ShapeDtypeStruct
+    outs = [sd((4, 2, 2, 48, n), BF) for n in cols] + [sd((4, 2, 2, 2) + down.shape, BF), sd((4, 2, 2, 2) + vec.shape, F32),
+            sd((8, 128, D), BF), sd((4, 128, D), BF), sd((8, 128, D), BF), sd((4, 128, D), BF)]
+    V, A = pl.BlockSpec(memory_space=pltpu.VMEM), pl.BlockSpec(memory_space=pl.ANY)
+    S = pltpu.SemaphoreType.DMA
+    return pl.pallas_call(
+        functools.partial(gather_kernel, cols),
+        out_shape=outs,
+        in_specs=[V, V, V, A, A, A, A],
+        out_specs=[A] * 9,
+        scratch_shapes=[pltpu.VMEM((2, 24, H), F32), pltpu.VMEM((24, H), F32), pltpu.VMEM((48, H), BF),
+                        S, S, S((5,)), S((5, 10)), S((5, 10)), S((2, 2, 3)), S((2, 8)), S((2, 4)), S((6,)), S((6,))],
+        compiler_params=pltpu.CompilerParams(collective_id=0, has_side_effects=True, vmem_limit_bytes=32 * 2**20),
+    )(qkv, out, up, down, vec, xin, cin)
+
+EPS = 1e-5
+NT = (((1,), (1,)), ((), ()))
+
+
+def nt(a, b):
+    return lax.dot_general(a, b, NT, preferred_element_type=F32)
+
+
+def nn(a, b):
+    return jnp.dot(a, b, preferred_element_type=F32)
+
+
+def rope_tables():
+    freq = np.exp(-math.log(10000.0) * (2.0 * np.arange(32, dtype=np.float32) / 64)).astype(np.float32)
+    ang = np.arange(1024, dtype=np.float32)[:, None] * freq[None, :]
+    c, s = np.cos(ang.astype(np.float64)), np.sin(ang.astype(np.float64))
+    return (np.concatenate([c, c, c, c], 1).astype(np.float32), np.concatenate([-s, s, -s, s], 1).astype(np.float32))
+
+
+def swap(u):
+    low = lax.broadcasted_iota(jnp.int32, u.shape, 1) % 64 < 32
+    return jnp.where(low, pltpu.roll(u, 96, 1), pltpu.roll(u, 32, 1))
+
+
+def norm(v):
+    mean = jnp.mean(v, axis=-1, keepdims=True)
+    cen = v - mean
+    inv = lax.rsqrt(jnp.mean(cen * cen, axis=-1, keepdims=True) + EPS)
+    return cen * inv, inv
+
+
+def norm_grad(e, n, inv, gain):
+    g = e * gain
+    return inv * (g - jnp.mean(g, axis=-1, keepdims=True) - n * jnp.mean(g * n, axis=-1, keepdims=True))
+
+
+def own_block(i, k):
+    return 2 * i + lax.rem(i + k, 2)
+
+
+def rows(i, n=128):
+    return pl.ds(pl.multiple_of(i * n, n), n)
+
+
+def spread(p):
+    low = lax.broadcasted_iota(jnp.int32, p.shape, 1) < 64
+    zero = jnp.zeros_like(p)
+    return jnp.concatenate([jnp.where(low, p, zero), jnp.where(low, zero, p)], axis=0)
+
+
+def pick(o):
+    low = lax.broadcasted_iota(jnp.int32, (128, 128), 0) < 64
+    return jnp.where(low, o[:, :128], o[:, 128:]).T
+
+
+def fill_bias(bias, is_long, k):
+    at = 0
+    for i in range(4):
+        kk = 256 * (i + 1)
+        key = lax.broadcasted_iota(jnp.int32, (kk, 256), 0)
+        q = own_block(i, k) * 128 + lax.broadcasted_iota(jnp.int32, (kk, 256), 1) % 128
+        first = jnp.where(is_long, 0, q - q % 256)
+        bias[at:at + kk, :] = jnp.where((key <= q) & (key >= first), 0.0, -1e30)
+        at += kk
+
+
+def attn_fwd(flag, XM, XA, wqkv, wout, gain, shift, bqkv, bout, COS, SIN,
+             acts, Q, K, V, att, lse, middle, bias, VT):
+    z, y, x, k = where_am_i()
+    is_long = flag[0] != 0
+    fill_bias(bias, is_long, k)
+    for j in range(8):
+        alt = jnp.logical_and(jnp.logical_not(is_long), lax.rem(jnp.int32(j), 2) != y)
+        blk = jnp.where(alt, XA[j // 2], XM[j]).astype(F32)
+        n, _ = norm(blk)
+        acts[j * 128:(j + 1) * 128, :] = (n * gain[...] + shift[...]).astype(BF)
+
+    def tables(j):
+        off = jnp.where(is_long, j, lax.rem(j, 2))
+        return COS[rows(off), :], SIN[rows(off), :]
+
+    @pl.loop(0, 8)
+    def _(j):
+        a = acts[rows(j), :]
+        c, s = tables(j)
+        for t in range(6):
+            u = nn(a, wqkv[:, 768 + t * 128:896 + t * 128]) + bqkv[:, 768 + t * 128:896 + t * 128]
+            K[rows(j), t * 128:(t + 1) * 128] = (u * c + swap(u) * s).astype(BF)
+        V[rows(j), :] = (nn(a, wqkv[:, 1536:]) + bqkv[:, 1536:]).astype(BF)
+
+    @pl.loop(0, 4)
+    def _(i):
+        j = own_block(i, k)
+        a = acts[rows(j), :]
+        c, s = tables(j)
+        for t in range(6):
+            u = nn(a, wqkv[:, t * 128:(t + 1) * 128]) + bqkv[:, t * 128:(t + 1) * 128]
+            Q[rows(i), t * 128:(t + 1) * 128] = (u * c + swap(u) * s).astype(BF) * jnp.asarray(0.125, BF)
+
+    @pl.loop(0, 6)
+    def _(h):
+        lanes = rows(h)
+        VT[...] = V[:, lanes].T
+        at = 0
+        for i in range(4):
+            kk = 256 * (i + 1)
+            qb = spread(Q[i * 128:(i + 1) * 128, lanes])
+            st = nt(K[0:kk, lanes], qb) + bias[at:at + kk, :]
+            top = jnp.max(st, axis=0, keepdims=True)
+            p = jnp.exp(st - top)
+            den = jnp.sum(p, axis=0, keepdims=True)
+            o = nn(VT[:, 0:kk], p.astype(BF)) * (1.0 / den)
+            att[i * 128:(i + 1) * 128, lanes] = pick(o)
+            lse[h, i:i + 1, :] = top + jnp.log(den)
+            at += kk
+
+    @pl.loop(0, 4)
+    def _(i):
+        j = own_block(i, k)
+        alt = jnp.logical_and(jnp.logical_not(is_long), lax.rem(j, 2) != y)
+        xb = jnp.where(alt, XA[i], XM[j]).astype(F32)
+        middle[rows(i), :] = xb + (nn(att[rows(i), :].astype(BF), wout[...]) + bout[...])
+
+
+def mlp(CH, flag, mix, middle, CM, CA, wup, wdown, gain, shift, bup, bdown,
+        block, gmid, gup, gdown, g_gain, g_shift, g_bup, g_bdown, mixsum, acts2, actsT, dg, ga, cf):
+    z, y, x, k = where_am_i()
+    is_long = flag[0] != 0
+    m5 = mix[5]
+    for i in range(4):
+        r = slice(i * 128, (i + 1) * 128)
+        mid = middle[r, :]
+        n, _ = norm(mid)
+        acts2[r, :] = (n * gain[...] + shift[...]).astype(BF)
+        j = own_block(jnp.int32(i), k)
+        alt = jnp.logical_and(jnp.logical_not(is_long), lax.rem(j, 2) != y)
+        c = jnp.where(alt, CA[i], CM[j]).astype(F32)
+        cf[r, :] = c
+        dg[r, :] = (m5 * c).astype(BF)
+        block[r, :] = mid + bdown[...]
+        ga[r, :] = jnp.zeros_like(mid)
+        actsT[:, r] = acts2[r, :].T
+    g_bdown[...] = jnp.sum(dg[...].astype(F32), axis=0, keepdims=True)
+
+    @pl.loop(0, wup.shape[1] // CH)
+    def _(f):
+        cols = rows(f, CH)
+        up = nn(acts2[...], wup[:, cols]) + bup[:, cols]
+        half_erf = 0.5 * lax.erf(up * (2.0 ** -0.5)) + 0.5
+        slope = half_erf + up * (jnp.exp(up * up * -0.5) * (1.0 / math.sqrt(2 * math.pi)))
+        act = (up * half_erf).astype(BF)
+        block[...] += nn(act, wdown[cols, :])
+        upg = (nt(dg[...], wdown[cols, :]) * slope).astype(BF)
+        g_bup[:, cols] = jnp.sum(upg.astype(F32), axis=0, keepdims=True)
+        gdown[cols, :] = nn(act.T, dg[...]).astype(BF)
+        gup[:, cols] = nn(actsT[...], upg).astype(BF)
+        ga[...] += nt(upg, wup[:, cols])
+
+    total = jnp.zeros((1, 768), F32)
+    gg = jnp.zeros((1, 768), F32)
+    gs = jnp.zeros((1, 768), F32)
+    for i in range(4):
+        r = slice(i * 128, (i + 1) * 128)
+        n, inv = norm(middle[r, :])
+        e = ga[r, :]
+        gg += jnp.sum(e * n, axis=0, keepdims=True)
+        gs += jnp.sum(e, axis=0, keepdims=True)
+        gmid[r, :] = m5 * cf[r, :] + norm_grad(e, n, inv, gain[...])
+        total += jnp.sum(cf[r, :] * block[r, :], axis=0, keepdims=True)
+    g_gain[...] = gg
+    g_shift[...] = gs
+    mixsum[...] = total
+
+
+def attn_bwd(flag, gmid, XM, XA, acts, Q, K, V, att, lse, wqkv, wout, gain, COS, SIN,
+             e, gqkv, gout, g_bqkv, g_bout, bias, KT, da, dQ, dK, dV, agrad, actsT, actsqT, KG, VG):
+    z, y, x, k = where_am_i()
+    is_long = flag[0] != 0
+    fill_bias(bias, is_long, k)
+    agrad[...] = gmid[...].astype(BF)
+    g_bout[...] = jnp.sum(agrad[...].astype(F32), axis=0, keepdims=True)
+
+    @pl.loop(0, 4)
+    def _(i):
+        da[rows(i), :] = nt(agrad[rows(i), :], wout[...]).astype(BF)
+
+    for t in range(6):
+        aT = att[:, t * 128:(t + 1) * 128].T.astype(BF)
+        gout[t * 128:(t + 1) * 128, :] = nn(aT, agrad[...]).astype(BF)
+    dK[...] = jnp.zeros_like(dK)
+    dV[...] = jnp.zeros_like(dV)
+
+    @pl.loop(0, 6)
+    def _(h):
+        lanes = rows(h)
+        KT[...] = K[:, lanes].T
+        at = 0
+        for i in range(4):
+            kk = 256 * (i + 1)
+            r = slice(i * 128, (i + 1) * 128)
+            d = da[r, lanes]
+            qb, db = spread(Q[r, lanes]), spread(d)
+            prod = (d.astype(F32) * att[r, lanes]).T
+            delta = jnp.concatenate([jnp.sum(prod[:64], axis=0, keepdims=True), jnp.sum(prod[64:], axis=0, keepdims=True)], axis=1)
+            st = nt(K[0:kk, lanes], qb) + bias[at:at + kk, :]
+            p = jnp.exp(st - lse[h, i:i + 1, :])
+            ds = (p * (nt(V[0:kk, lanes], db) - delta)).astype(BF)
+            dV[0:kk, lanes] += nn(p.astype(BF), db)
+            dK[0:kk, lanes] += nn(ds, qb)
+            dQ[r, lanes] = pick(nn(KT[:, 0:kk], ds)) * 0.125
+            at += kk
+
+    def tables(j):
+        off = jnp.where(is_long, j, lax.rem(j, 2))
+        return COS[rows(off), :], SIN[rows(off), :]
+
+    for j in range(8):
+        actsT[:, j * 128:(j + 1) * 128] = acts[j * 128:(j + 1) * 128, :].T
+    for i in range(4):
+        j = own_block(jnp.int32(i), k)
+        actsqT[:, i * 128:(i + 1) * 128] = acts[rows(j), :].T
+        c, s = tables(j)
+        for t in range(6):
+            u = dQ[i * 128:(i + 1) * 128, t * 128:(t + 1) * 128]
+            da[i * 128:(i + 1) * 128, t * 128:(t + 1) * 128] = (u * c - swap(u) * s).astype(BF)
+
+    @pl.loop(0, 8)
+    def _(j):
+        c, s = tables(j)
+        for t in range(6):
+            u = dK[rows(j), t * 128:(t + 1) * 128]
+            KG[rows(j), t * 128:(t + 1) * 128] = (u * c - swap(u) * s).astype(BF)
+        VG[rows(j), :] = dV[rows(j), :].astype(BF)
+        e[rows(j), :] = nt(KG[rows(j), :], wqkv[:, 768:1536]) + nt(VG[rows(j), :], wqkv[:, 1536:])
+
+    @pl.loop(0, 4)
+    def _(i):
+        j = own_block(i, k)
+        e[rows(j), :] += nt(da[rows(i), :], wqkv[:, :768])
+
+    g_bqkv[:, :768] = jnp.sum(da[...].astype(F32), axis=0, keepdims=True)
+    g_bqkv[:, 768:1536] = jnp.sum(KG[...].astype(F32), axis=0, keepdims=True)
+    g_bqkv[:, 1536:] = jnp.sum(VG[...].astype(F32), axis=0, keepdims=True)
+
+    @pl.loop(0, 6)
+    def _(t):
+        gqkv[rows(t), :768] = nn(actsqT[rows(t), :], da[...]).astype(BF)
+        gqkv[rows(t), 768:1536] = nn(actsT[rows(t), :], KG[...]).astype(BF)
+        gqkv[rows(t), 1536:] = nn(actsT[rows(t), :], VG[...]).astype(BF)
+
+
+sd = jax.ShapeDtypeStruct
+VM = pltpu.VMEM
+vs = pl.BlockSpec(memory_space=pltpu.VMEM)
+ss = pl.BlockSpec(memory_space=pltpu.SMEM)
+CP = pltpu.CompilerParams(vmem_limit_bytes=60 * 2**20)
+
+
+def attn_fwd_call(flag, *ins):
+    return pl.pallas_call(attn_fwd,
+        out_shape=[sd((1024, 768), BF), sd((512, 768), BF), sd((1024, 768), BF), sd((1024, 768), BF),
+                   sd((512, 768), F32), sd((6, 4, 256), F32), sd((512, 768), F32)],
+        in_specs=[ss] + [vs] * len(ins), out_specs=[vs] * 7,
+        scratch_shapes=[VM((2560, 256), F32), VM((128, 1024), BF)],
+        compiler_params=CP)(flag, *ins)
+
+
+def mlp_call(flag, mix, *ins):
+    r = sd((1, 768), F32)
+    return pl.pallas_call(functools.partial(mlp, 512),
+        out_shape=[sd((512, 768), F32), sd((512, 768), F32), sd((768, 3072), BF), sd((3072, 768), BF), r, r, sd((1, 3072), F32), r, r],
+        in_specs=[ss, ss] + [vs] * len(ins), out_specs=[vs] * 9,
+        scratch_shapes=[VM((512, 768), BF), VM((768, 512), BF), VM((512, 768), BF), VM((512, 768), F32), VM((512, 768), F32)],
+        compiler_params=CP)(flag, mix, *ins)
+
+
+def attn_bwd_call(flag, *ins):
+    return pl.pallas_call(attn_bwd,
+        out_shape=[sd((1024, 768), F32), sd((768, 2304), BF), sd((768, 768), BF), sd((1, 2304), F32), sd((1, 768), F32)],
+        in_specs=[ss] + [vs] * len(ins), out_specs=[vs] * 5,
+        scratch_shapes=[VM((2560, 256), F32), VM((128, 1024), BF), VM((512, 768), BF), VM((512, 768), F32), VM((1024, 768), F32),
+                        VM((1024, 768), F32), VM((512, 768), BF), VM((768, 1024), BF), VM((768, 512), BF), VM((1024, 768), BF), VM((1024, 768), BF)],
+        compiler_params=CP)(flag, *ins)
+
+
+class Scatter:
+    STAGES = 5
+
+    def __init__(self, part, PA, RA, RB, RC, RZ, put, send, recv, pos):
+        self.__dict__.update(locals())
+        z, y, x, k = pos
+        self.own = (y, x)
+        self.p2 = jnp.where(k == 0, 1 - y, y), jnp.where(k == 0, x, 1 - x)
+        self.p3 = jnp.where(k == 0, y, 1 - y), jnp.where(k == 0, 1 - x, x)
+        self.d4 = 1 - y, 1 - x
+        blk = lambda yx: PA.at[:, yx[0], yx[1]]
+        n3, n2 = dev(z, *self.p3, k), dev(z, *self.p2, k)
+        self.pre = remote(part(slice(None), slice(None), slice(None), 1 - k), RA, send.at[0], recv.at[0], dev(z, y, x, 1 - k))
+        self.b1 = remote(blk(self.d4), RB.at[1], send.at[1], recv.at[1], n3)
+        self.b0 = remote(blk(self.p3), RB.at[0], send.at[2], recv.at[2], n3)
+        self.c = remote(blk(self.p2), RC, send.at[3], recv.at[3], n2)
+        self.zs = [remote(PA.at[lax.rem(z + d, 4), y, x], RZ.at[d - 1], send.at[3 + d], recv.at[3 + d],
+                          dev(lax.rem(z + d, 4), y, x, k)) for d in (1, 2, 3)]
+
+    def add(self, yx, other):
+        @pl.loop(0, 4)
+        def _(i):
+            a = self.PA[i, yx[0], yx[1]].astype(F32) + other[i].astype(F32)
+            self.PA[i, yx[0], yx[1]] = a.astype(BF)
+
+    def first(self, yx):
+        k = self.pos[3]
+        @pl.loop(0, 4)
+        def _(i):
+            a = self.part(i, yx[0], yx[1], k)[...].astype(F32) + self.RA[i, yx[0], yx[1]].astype(F32)
+            self.PA[i, yx[0], yx[1]] = a.astype(BF)
+
+    def stage(self, n):
+        z, y, x, k = self.pos
+        if n == 0:
+            self.pre.start()
+        elif n == 1:
+            self.pre.wait_recv()
+            self.first(self.d4)
+            self.b1.start()
+            self.first(self.p3)
+            self.b0.start()
+            self.first(self.p2)
+            self.first(self.own)
+        elif n == 2:
+            self.b1.wait_recv()
+            self.add(self.p2, self.RB.at[1])
+            self.c.start()
+            self.b0.wait_recv()
+            self.add(self.own, self.RB.at[0])
+        elif n == 3:
+            self.c.wait_recv()
+            self.add(self.own, self.RC)
+            for c in self.zs: c.start()
+        elif n == 4:
+            for c in self.zs: c.wait_recv()
+            tot = self.PA[z, y, x].astype(F32)
+            for i in range(3):
+                tot = tot + self.RZ[i].astype(F32)
+            self.put(tot)
+            for c in [self.pre, self.b0, self.b1, self.c] + self.zs: c.wait_send()
+
+
+def reduce_kernel(cols, flag, gqkv, gout, gup, gdown, e, gmid, block, XM, XA, gain, vin,
+                  oq, oo, ou, od, vout, H0, HL, HS,
+                  PQ, AQ, BQ, CQ, ZQ, PO, AO, BO, CO, ZO, PU, AU, BU, CU, ZU, PD, AD, BD, CD, ZD,
+                  fin, fsib, es, er, gx, bl, vbuf, vrec,
+                  ssem, rsem, hsend, h0, hl, hs, misc_s, misc_r, vsend, vrecv):
+    pos = z, y, x, k = where_am_i()
+    is_long = flag[0] != 0
+    greet(z, y, x, k)
+    sib = dev(z, y, x, 1 - k)
+    for i in range(4):
+        es[i] = e[rows(own_block(jnp.int32(i), 1 - k)), :].astype(BF)
+    ecp = remote(es, er, misc_s.at[0], misc_r.at[0], sib)
+    ecp.start()
+    halves = [c // 2 for c in cols]
+
+    def colpart(W, half):
+        def f(zz, yy, xx, kk):
+            return W.at[zz, yy, xx, :, pl.ds(pl.multiple_of(kk * half, 128), half)]
+        return f
+    offs = [0, halves[0], halves[0] + halves[1]]
+    def put_cols(i):
+        def put(t):
+            fin[0, :, offs[i]:offs[i] + halves[i]] = t[:24]
+            fin[1, :, offs[i]:offs[i] + halves[i]] = t[24:]
+        return put
+    def put_down(t):
+        od[...] = t
+    S = lambda a, part, bufs, put: Scatter(part, *bufs, put, ssem.at[a], rsem.at[a], pos)
+    gs = [S(0, lambda zz, yy, xx, kk: gdown.at[zz, yy, xx, kk], (PD, AD, BD, CD, ZD), put_down),
+          S(1, colpart(gup, halves[2]), (PU, AU, BU, CU, ZU), put_cols(2)),
+          S(2, colpart(gout, halves[1]), (PO, AO, BO, CO, ZO), put_cols(1)),
+          S(3, colpart(gqkv, halves[0]), (PQ, AQ, BQ, CQ, ZQ), put_cols(0))]
+    homes = []
+    g = z
+    def send_home(a, buf):
+        for i in range(4):
+            j = own_block(jnp.int32(i), k)
+            yj = lax.rem(j, 2)
+            zj = jnp.int32(i)
+            core = g // 2
+            straight = yj == y
+            slot = lax.rem(g, 2)
+            for n, (dst, rs, yd, cond) in enumerate((
+                (H0.at[a, slot], h0.at[a, slot], y, straight),
+                (HL.at[a, slot], hl.at[a, slot], 1 - y, jnp.logical_not(straight)),
+                (HS.at[a, slot], hs.at[a, slot], y, jnp.logical_not(straight)))):
+                me = (zj == z) & (yd == y) & (core == k)
+                cp = remote(buf.at[i], dst, hsend.at[a, i, n], rs, dev(zj, yd, x, core))
+                @pl.when(cond & me)
+                def _():
+                    pltpu.make_async_copy(buf.at[i], dst, rs).start()
+                @pl.when(cond & jnp.logical_not(me))
+                def _():
+                    cp.start()
+                homes.append((cp, cond & jnp.logical_not(me)))
+    for i in range(4):
+        bl[i] = block[i * 128:(i + 1) * 128, :].astype(BF)
+    send_home(0, bl)
+
+    def token_grads():
+        ecp.wait_recv()
+        gg = jnp.zeros((1, 768), F32)
+        gsh = jnp.zeros((1, 768), F32)
+        for i in range(4):
+            j = own_block(jnp.int32(i), k)
+            alt = jnp.logical_and(jnp.logical_not(is_long), lax.rem(j, 2) != y)
+            n, inv = norm(jnp.where(alt, XA[i], XM[j]).astype(F32))
+            ee = e[rows(j), :] + er[i].astype(F32)
+            gg += jnp.sum(ee * n, axis=0, keepdims=True)
+            gsh += jnp.sum(ee, axis=0, keepdims=True)
+            gx[i] = (gmid[i * 128:(i + 1) * 128, :] + norm_grad(ee, n, inv, gain[...])).astype(BF)
+        send_home(1, gx)
+        vbuf[0] = vin[...]
+        for t in range(6):
+            vbuf[0, t:t + 1, :] = gg[:, t * 128:(t + 1) * 128]
+            vbuf[0, 6 + t:7 + t, :] = gsh[:, t * 128:(t + 1) * 128]
+
+    sc = gs[0]
+    vec_steps = [[sib], [dev(z, *sc.p2, k)], [dev(z, *sc.p3, k)], [dev(lax.rem(z + d, 4), y, x, k) for d in (1, 2, 3)]]
+    vcp = []
+    def vec_stage(n):
+        if n > 0:
+            for c in vcp[-1]: c.wait_recv()
+            t = vbuf[n - 1]
+            for r in range(len(vcp[-1])):
+                t = t + vrec[n - 1 + r]
+            if n < 4: vbuf[n] = t
+            else: vout[...] = t
+        if n < 4:
+            vcp.append([remote(vbuf.at[n], vrec.at[n + i], vsend.at[n + i], vrecv.at[n + i], d) for i, d in enumerate(vec_steps[n])])
+            for c in vcp[-1]: c.start()
+
+    for tick in range(len(gs) + Scatter.STAGES - 1):
+        for i, gg_ in enumerate(gs):
+            n = tick - i
+            if 0 <= n < Scatter.STAGES:
+                gg_.stage(n)
+        if tick == 0:
+            token_grads()
+        if 1 <= tick <= 5:
+            vec_stage(tick - 1)
+    lst = remote(fin.at[1 - k], fsib, misc_s.at[1], misc_r.at[1], sib)
+    lst.start()
+    lst.wait_recv()
+    for i, o in enumerate((oq, oo, ou)):
+        mine = fin[k, :, offs[i]:offs[i] + halves[i]]
+        theirs = fsib[:, offs[i]:offs[i] + halves[i]]
+        o[:, :halves[i]] = jnp.where(k == 0, mine, theirs)
+        o[:, halves[i]:] = jnp.where(k == 0, theirs, mine)
+    for a in range(2):
+        for i in range(2):
+            remote(H0.at[a, i], H0.at[a, i], hsend.at[0, 0, 0], h0.at[a, i], sib).wait_recv()
+            remote(HL.at[a, i], HL.at[a, i], hsend.at[0, 0, 0], hl.at[a, i], sib).wait_recv()
+            remote(HS.at[a, i], HS.at[a, i], hsend.at[0, 0, 0], hs.at[a, i], sib).wait_recv()
+    lst.wait_send()
+    ecp.wait_send()
+    for cs in vcp:
+        for c in cs: c.wait_send()
+    for cp, cond in homes:
+        @pl.when(cond)
+        def _():
+            cp.wait_send()
+
+
+def reduce_call(flag, gqkv, gout, gup, gdown, *ins):
+    cols = (gqkv.shape[1], gout.shape[1], gup.shape[1])
+    gqkv, gout, gup = (g.reshape(4, 2, 2, 48, g.shape[1]) for g in (gqkv, gout, gup))
+    gdown = gdown.reshape(4, 2, 2, 2, 96, 768)
+    any_ = pl.BlockSpec(memory_space=pl.ANY)
+    bufs = []
+    for r, n in ((48, cols[0] // 2), (48, cols[1] // 2), (48, cols[2] // 2), (96, 768)):
+        bufs += [VM((4, 2, 2, r, n), BF), VM((4, 2, 2, r, n), BF), VM((2, 4, r, n), BF), VM((4, r, n), BF), VM((3, r, n), BF)]
+    H = sum(cols) // 2
+    DS = pltpu.SemaphoreType.DMA
+    home = sd((2, 2, 128, 768), BF)
+    return pl.pallas_call(functools.partial(reduce_kernel, cols),
+        out_shape=[sd((24, cols[0]), F32), sd((24, cols[1]), F32), sd((24, cols[2]), F32), sd((96, 768), F32), sd((80, 128), F32), home, home, home],
+        in_specs=[ss] + [vs] * (4 + len(ins)), out_specs=[vs] * 5 + [any_] * 3,
+        scratch_shapes=bufs + [VM((2, 24, H), F32), VM((24, H), F32), VM((4, 128, 768), BF), VM((4, 128, 768), BF), VM((4, 128, 768), BF),
+                               VM((4, 128, 768), BF), VM((4, 80, 128), F32), VM((6, 80, 128), F32),
+                               DS((4, 7)), DS((4, 7)), DS((2, 4, 3)), DS((2, 2)), DS((2, 2)), DS((2, 2)), DS((2,)), DS((2,)), DS((6,)), DS((6,))],
+        compiler_params=pltpu.CompilerParams(collective_id=1, has_side_effects=True, vmem_limit_bytes=62 * 2**20),
+    )(flag, gqkv, gout, gup, gdown, *ins)
+
+def fast_shards(inputs, history, seq_lengths, attn_gain, attn_shift, qkv_weight, qkv_bias, out_weight, out_bias, mlp_gain,
+                mlp_shift, up_weight, up_bias, down_weight, down_bias, mix_weights, cotangent):
+    seq, batch = lax.axis_index("seq"), lax.axis_index("batch")
+    z, y, x, k = seq // 2, seq % 2, batch // 2, batch % 2
+    vectors = (attn_gain, attn_shift, qkv_bias, out_bias, mlp_gain, mlp_shift, up_bias, down_bias)
+    packed = jnp.concatenate([v.astype(F32) for v in vectors] + [seq_lengths.astype(F32)])
+    packed = jnp.pad(packed, (0, 1024 - packed.shape[0])).reshape(8, 128)
+    QKV, OUT, UP, DOWN, VEC, XM, XA, CM, CA = gather_call(qkv_weight, out_weight, up_weight, down_weight, packed, inputs, cotangent)
+    wqkv, wout, wup = (w.reshape(768, w.shape[-1]) for w in (QKV, OUT, UP))
+    wdown = DOWN.reshape(3072, 768)
+    flat = VEC.reshape(32, 1024)
+    full, at = [], 0
+    for v in vectors:
+        n = v.shape[0]
+        full.append(flat[:, at:at + n].reshape(1, 32 * n))
+        at += n
+    a_gain, a_shift, bqkv, bout, m_gain, m_shift, bup, bdown = full
+    length = VEC[0, 0, :, :, 0, :].reshape(2, 2, 0 + 128)[:, :, 0] if False else flat[:4, at:at + 2].reshape(2, 4)
+    lens = lax.dynamic_index_in_dim(length, x, 0, keepdims=False)
+    flag = (lax.dynamic_index_in_dim(lens, z, 0, keepdims=True) == LONG_LEN).astype(jnp.int32)
+    COS, SIN = (jnp.asarray(t) for t in rope_tables())
+    acts, Q, K, V, att, lse, middle = attn_fwd_call(flag, XM, XA, wqkv, wout, a_gain, a_shift, bqkv, bout, COS, SIN)
+    block, gmid, gup, gdown, g_mgain, g_mshift, g_bup, g_bdown, mixsum = mlp_call(
+        flag, mix_weights, middle, CM, CA, wup, wdown, m_gain, m_shift, bup, bdown)
+    e, gqkv, gout, g_bqkv, g_bout = attn_bwd_call(flag, gmid, XM, XA, acts, Q, K, V, att, lse, wqkv, wout, a_gain, COS, SIN)
+    earlier, cot = history.astype(F32), cotangent.astype(F32)
+    mix_terms = jnp.concatenate([jnp.sum(earlier * cot[None], axis=(1, 2, 3)), jnp.sum(mixsum)[None]])
+    grad_history = (mix_weights[:-1, None, None, None] * cot[None]).astype(BF)
+    vin = jnp.concatenate([jnp.zeros((1536,), F32)] + [v.reshape(-1) for v in (g_bqkv, g_bout, g_mgain, g_mshift, g_bup, g_bdown)]
+                          + [mix_terms, jnp.zeros((250,), F32)]).reshape(80, 128)
+    oq, oo, ou, od, vout, H0, HL, HS = reduce_call(flag, gqkv, gout, gup, gdown, e, gmid, block, XM, XA, a_gain, vin)
+    is_long = (seq_lengths == LONG_LEN)[None, :, None, None]
+    other = jnp.where(is_long, HL, HS)
+    home = jnp.where(y == 0, jnp.concatenate([H0, other], axis=2), jnp.concatenate([other, H0], axis=2))
+    layer_out = (jnp.sum(mix_weights[:-1, None, None, None] * earlier, axis=0) + mix_weights[-1] * home[0].astype(F32)).astype(BF)
+    vflat = vout.reshape(-1)
+    me = seq * 4 + batch
+    gv, at = [], 0
+    for v in vectors:
+        n = v.shape[0]
+        gv.append(lax.dynamic_slice_in_dim(vflat, at + me * n, n, 0))
+        at += 32 * n
+    grad_mix = vflat[at:at + 6]
+    return (layer_out, home[1], grad_history, gv[0], gv[1], oq, gv[2], oo, gv[3], gv[4], gv[5], ou, gv[6], od, gv[7], grad_mix)
+
+
+def fits(mesh, inputs):
+    shape = dict(mesh.shape)
+    return shape == {"seq": 8, "batch": 4} and inputs.shape == (8, 2048, 768)
+
+
+def solution(mesh):
+    def run(*args):
+        body = fast_shards if fits(mesh, args[0]) else shards
+        return placed(mesh, body)(*args)
+    return run

time: 1400 us -> 399 us (0.28)
  waiting for transfers between devices: 961 us -> 0 us
  Pallas kernels: 0 us -> 343 us
  matrix products: 138 us -> 0 us
  blocking collectives: 93.6 us -> 0 us
  local copies, waits for them, and re-layouts: 99.9 us -> 39.7 us
  other arithmetic: 58.5 us -> 13.7 us
  loops' own time: 21.9 us -> 0 us
  between operations: 17.2 us -> 1.57 us
    reduce_scatter x6 -> x0, waiting for transfers between devices: 590 us -> none  [the longest x2 177 us: shards(): lax.psum_scatter(blocks.reshape(lax.axis_size('seq') * tok_count, 2 * mod...]
    all_gather x8 -> x0, waiting for transfers between devices: 368 us -> none  [the longest x2 110 us: shards(): lax.all_gather(key_flat, 'seq', axis=0, tiled=True)]
    pallas_call x0 -> x5, Pallas kernels: none -> 343 us  [the longest x1 133 us: gather_call(): pl.pallas_call(functools.partial(gather_kernel, cols), out_shape=outs, in...]
    dot_general x38 -> x0, matrix products: 138 us -> none  [the longest x2 22.9 us: shards(): jnp.einsum('td,fd->tf', down_grad_b, back_down, preferred_element_type=jn...]
    unnamed x2 -> x0, blocking collectives: 93.6 us -> none
    dynamic_slice x30 -> x4, local copies, waits for them, and re-layouts: 27.5 us -> 4.53 us  [the longest x3 3.94 us: fast_shards(): gv.append(lax.dynamic_slice_in_dim(vflat, at + me * n, n, 0))]
    another operation x30 -> x0, loops' own time: 21.9 us -> none  [the longest x2 5.85 us: attend_rows(): lax.scan(one_block, current, jnp.arange(key_count // block_rows, dtype=jn...]
    reduce_sum x14 -> x2, other arithmetic: 23.7 us -> 6.26 us  [the longest x1 5.65 us: fast_shards(): jnp.sum(earlier * cot[None], axis=(1, 2, 3))]
  transfers between devices with their start and end apart: 14 -> 0, of which waited for: 14 -> 0; matrix products, arithmetic and copies ran while one was open for 15% -> 0% of each run, Pallas kernels for 0% -> 0%
where the time goes in v1:
time: 399 us; the launch traced here: 398 us
  Pallas kernels  343 us (86%)
  local copies, waits for them, and re-layouts  39.7 us (10%)
  other arithmetic  13.7 us (3%)
    pallas_call x1, Pallas kernels, gather_call(): pl.pallas_call(functools.partial(gather_kernel, cols), out_shape=outs, in...  133 us
    pallas_call x1, Pallas kernels, reduce_call(): pl.pallas_call(functools.partial(reduce_kernel, cols), out_shape=[sd((24,...  114 us
    pallas_call x1, Pallas kernels, attn_bwd_call(): pl.pallas_call(attn_bwd, out_shape=[sd((1024, 768), F32), sd((768, 2304),...  40.4 us
    pallas_call x1, Pallas kernels, attn_fwd_call(): pl.pallas_call(attn_fwd, out_shape=[sd((1024, 768), BF), sd((512, 768), B...  28.4 us
    pallas_call x1, Pallas kernels, mlp_call(): pl.pallas_call(functools.partial(mlp, 512), out_shape=[sd((512, 768), F32...  26.8 us
    unnamed x57, local copies, waits for them, and re-layouts  19.9 us

profile of v1, /device:TPU:0, one launch (start us, length us, event | category | flops | bytes accessed | tf_op | source)
XLA Modules:
  0.0 397.7 jit_solution(16805895935177710042)
XLA Ops:
  1.3 5.4 %concatenate.12 = f32[314]{0:T(512)S(1)} concatenate(bf16[24]{0:T(256)(128)(2,1)} %param.22, bf16[24]{0:T(256)(128)(2,1)} %param.23, bf16[72]{0:T(256)(128)(2,1)} %param.25, bf16[24]{0:T(256)(128)(2,1)} %param.27, bf16[24]{0:T(256)(128)(2,1)} %param.28, bf16[24]{0:T(256)(128)(2,1)} %param.29, bf16[96]{0:T(256)(128)(2,1)} %param.31, bf16[24]{0:T(256)(128)(2,1)} %param.33, ...), dimensions={0} | concatenate | bytes 1888 | tf_op jit(solution)/shard_map/concatenate | solution.py:1264
  6.8 1.1 copy-done.6
  7.9 1.1 copy-done.9
  9.0 0.9 copy-done.11
  10.0 0.9 copy-done.12
  10.9 0.9 copy-done.13
  11.8 0.8 copy-done.14
  12.5 133.2 %shard_map.306 = (bf16[4,2,2,48,2304]{4,3,2,1,0:T(8,128)(2,1)S(1)}, bf16[4,2,2,48,768]{4,3,2,1,0:T(8,128)(2,1)S(1)}, bf16[4,2,2,48,3072]{4,3,2,1,0:T(8,128)(2,1)...) custom-call(bf16[24,2304]{1,0:T(8,128)(2,1)S(1)} %copy-done.13, ...), custom_call_target="tpu_custom_call" | custom-call | tf_op jit(solution)/shard_map/pallas_call | solution.py:757
  145.7 1.2 copy-done
  146.9 1.8 copy-done.1
  148.7 0.9 copy-done.2
  149.5 1.0 copy-done.3
  150.6 2.2 copy-done.4
  152.8 2.1 copy-done.5
  154.9 1.2 copy-done.8
  156.1 0.9 copy-done.10
  161.3 28.4 %shard_map.307 = (bf16[1024,768]{1,0:T(8,128)(2,1)}, bf16[512,768]{1,0:T(8,128)(2,1)}, bf16[1024,768]{1,0:T(8,128)(2,1)}, bf16[1024,768]{1,0:T(8,128)(2,1)}, f32...) custom-call(s32[1]{0:T(128)} %bitcast.2.flag, bf16[8,128,768]{2,1,0:T(8,128)(2,1)} %copy-done, ...), custom_call_target="tpu_custom_call" | custom-call | tf_op jit(solution)/shard_map/pallas_call | solution.py:1026
  192.5 26.8 %shard_map.308 = (f32[512,768]{1,0:T(8,128)}, f32[512,768]{1,0:T(8,128)}, bf16[768,3072]{1,0:T(8,128)(2,1)}, bf16[3072,768]{1,0:T(8,128)(2,1)}, f32[1,768]{1,0:T...) custom-call(s32[1]{0:T(128)} %bitcast.2.flag, f32[6]{0:T(128)} %mix.1, ...), custom_call_target="tpu_custom_call" | custom-call | tf_op jit(solution)/shard_map/pallas_call | solution.py:1036
  219.4 40.4 %shard_map.309 = (f32[1024,768]{1,0:T(8,128)}, bf16[768,2304]{1,0:T(8,128)(2,1)}, bf16[768,768]{1,0:T(8,128)(2,1)}, f32[1,2304]{1,0:T(1,128)}, f32[1,768]{1,0:T(1,128)}) custom-call(s32[1]{0:T(128)} %bitcast.2.flag, f32[512,768]{1,0:T(8,128)} %get-tuple-element.64.gmid, bf16[8,128,768]{2,1,0:T(8,128)(2,1)} %copy-done, bf16[4,128,768]{2,1,0:T(8,128)(2,1)} %copy-done.2, ...), custom_call_target="tpu_custom_call" | custom-call | tf_op jit(solution)/shard_map/pallas_call | solution.py:1044
  259.8 0.7 reduce
  262.1 5.7 %fusion.1 = (f32[5]{0:T(128)S(1)}, f32[2,256,768]{2,1,0:T(8,128)S(1)}, bf16[5,2,256,768]{3,2,1,0:T(8,128)(2,1)}) fusion(bf16[5,2,256,768]{3,2,1,0:T(8,128)(2,1)} %param.20, f32[2,256,768]{2,1,0:T(8,128)S(1)} %convert_element_type.62, f32[5]{0:T(128)S(1)} %bitcast.45), kind=kLoop, calls=%fused_computation.3 | loop fusion | flops 13369339 | bytes 11010088 | tf_op jit(solution)/shard_map/reduce_sum | solution.py:1285
  267.8 1.3 concatenate.13
  269.1 114.0 %shard_map.310 = (f32[24,2304]{1,0:T(8,128)}, f32[24,768]{1,0:T(8,128)}, f32[24,3072]{1,0:T(8,128)}, f32[96,768]{1,0:T(8,128)}, f32[80,128]{1,0:T(8,128)}, /*ind...) custom-call(s32[1]{0:T(128)} %bitcast.2.flag, ...), custom_call_target="tpu_custom_call" | custom-call | tf_op jit(solution)/shard_map/pallas_call | solution.py:1250
  383.2 1.5 broadcast_select_fusion
  384.7 1.9 maximum_select_fusion
  387.2 1.7 fusion.2
  388.9 0.9 slice_bitcast_fusion
  389.9 1.4 fusion.4
  391.2 1.3 dynamic_slice.33
  392.5 1.3 dynamic_slice.37
  393.8 1.2 slice.68
  397.0 0.7 copy.45
  (68 shorter events, 11.3 us)
Async XLA Ops:
  6.8 1.1 copy-start.6
  7.9 1.1 copy-start.9
  9.0 0.9 copy-start.11
  9.9 0.9 copy-start.12
  10.9 0.9 copy-start.13
  11.8 0.8 copy-start.14
  145.7 1.2 copy-start
  146.9 1.8 copy-start.1
  148.7 0.9 copy-start.2
  149.5 1.0 copy-start.3
  150.6 2.2 copy-start.4
  152.8 2.1 copy-start.5
  154.9 1.2 copy-start.8
  156.1 0.9 copy-start.10
  219.3 41.9 %copy-start.23 = (f32[1,768]{1,0:T(1,128)S(1)}, f32[1,768]{1,0:T(1,128)}, u32[]{:S(2)}) copy-start(f32[1,768]{1,0:T(1,128)} %get-tuple-element.79) | copy-start | bytes 9220
  219.3 42.0 %copy-start.22 = (f32[1,768]{1,0:T(1,128)S(1)}, f32[1,768]{1,0:T(1,128)}, u32[]{:S(2)}) copy-start(f32[1,768]{1,0:T(1,128)} %get-tuple-element.80) | copy-start | bytes 9220
  219.3 42.0 %copy-start.21 = (f32[1,768]{1,0:T(1,128)S(1)}, f32[1,768]{1,0:T(1,128)}, u32[]{:S(2)}) copy-start(f32[1,768]{1,0:T(1,128)} %get-tuple-element.82) | copy-start | bytes 9220
  219.3 42.0 %copy-start.20 = (f32[1,768]{1,0:T(1,128)S(1)}, f32[1,768]{1,0:T(1,128)}, u32[]{:S(2)}) copy-start(f32[1,768]{1,0:T(1,128)} %get-tuple-element.83) | copy-start | bytes 9220
  219.4 42.6 %copy-start.7 = (bf16[2,256,768]{2,1,0:T(8,128)(2,1)S(1)}, bf16[2,256,768]{2,1,0:T(8,128)(2,1)}, u32[]{:S(2)}) copy-start(bf16[2,256,768]{2,1,0:T(8,128)(2,1)} %cin.1) | copy-start | bytes 2359300
  259.8 2.3 copy-start.24
  262.1 5.7 %copy-start.19 = (f32[1,3072]{1,0:T(1,128)S(1)}, f32[1,3072]{1,0:T(1,128)}, u32[]{:S(2)}) copy-start(f32[1,3072]{1,0:T(1,128)} %get-tuple-element.81) | copy-start | bytes 36868
  269.1 114.0 %copy-start.25 = (s32[2]{0:T(128)S(1)}, s32[2]{0:T(128)}, u32[]{:S(2)}) copy-start(s32[2]{0:T(128)} %param.21) | copy-start | bytes 28
  388.9 6.1 %copy-start.17 = (f32[24,2304]{1,0:T(8,128)S(1)}, f32[24,2304]{1,0:T(8,128)}, u32[]{:S(2)}) copy-start(f32[24,2304]{1,0:T(8,128)} %get-tuple-element.128) | copy-start | bytes 663556
  388.9 6.8 %copy-start.18 = (f32[24,768]{1,0:T(8,128)S(1)}, f32[24,768]{1,0:T(8,128)}, u32[]{:S(2)}) copy-start(f32[24,768]{1,0:T(8,128)} %get-tuple-element.130) | copy-start | bytes 221188
  388.9 7.4 %copy-start.16 = (f32[24,3072]{1,0:T(8,128)S(1)}, f32[24,3072]{1,0:T(8,128)}, u32[]{:S(2)}) copy-start(f32[24,3072]{1,0:T(8,128)} %get-tuple-element.134) | copy-start | bytes 884740
  388.9 8.1 %copy-start.15 = (f32[96,768]{1,0:T(8,128)S(1)}, f32[96,768]{1,0:T(8,128)}, u32[]{:S(2)}) copy-start(f32[96,768]{1,0:T(8,128)} %get-tuple-element.136) | copy-start | bytes 884740

commit v2 on v1

--- a/solution.py
+++ b/solution.py
@@ -938,7 +938,7 @@
     mixsum[...] = total
 
 
-def attn_bwd(flag, gmid, XM, XA, acts, Q, K, V, att, lse, wqkv, wout, gain, COS, SIN,
+def attn_bwd(flag, gmid, acts, Q, K, V, att, lse, wqkv, wout, COS, SIN,
              e, gqkv, gout, g_bqkv, g_bout, bias, KT, da, dQ, dK, dV, agrad, actsT, actsqT, KG, VG):
     z, y, x, k = where_am_i()
     is_long = flag[0] != 0
@@ -1047,6 +1047,338 @@
         scratch_shapes=[VM((2560, 256), F32), VM((128, 1024), BF), VM((512, 768), BF), VM((512, 768), F32), VM((1024, 768), F32),
                         VM((1024, 768), F32), VM((512, 768), BF), VM((768, 1024), BF), VM((768, 512), BF), VM((1024, 768), BF), VM((1024, 768), BF)],
         compiler_params=CP)(flag, *ins)
+
+
+VROWS = (24, 24, 72, 24, 24, 24, 96, 24)
+
+
+def widen(vecs, row, n):
+    v = vecs[:, row, :].astype(BF)
+    wide = 32 * n
+    j = lax.broadcasted_iota(jnp.int32, (128, wide), 1)
+    i = lax.broadcasted_iota(jnp.int32, (128, wide), 0)
+    q = jnp.floor((j.astype(F32) + 0.5) * (1.0 / n)).astype(jnp.int32)
+    hot = jnp.where(j - q * n == i, 1.0, 0.0).astype(BF)
+    full = nn(v, hot)
+    d = lax.broadcasted_iota(jnp.int32, (32, wide), 0)
+    return jnp.sum(jnp.where(q[:32] == d, full, 0.0), axis=0, keepdims=True)
+
+
+def lane(tile, row, at):
+    r = lax.broadcasted_iota(jnp.int32, tile.shape, 0)
+    c = lax.broadcasted_iota(jnp.int32, tile.shape, 1)
+    v = jnp.sum(jnp.where((r == row) & (c == at), tile, 0.0), axis=1, keepdims=True)
+    return jnp.sum(v, axis=0, keepdims=True)
+
+
+def longer(length, shape):
+    return jnp.broadcast_to(length, shape) > 512.0
+
+
+def bias_rows(bias, length, k):
+    at = 0
+    for i in range(4):
+        kk = 256 * (i + 1)
+        key = lax.broadcasted_iota(jnp.int32, (kk, 256), 0)
+        q = own_block(i, k) * 128 + lax.broadcasted_iota(jnp.int32, (kk, 256), 1) % 128
+        first = jnp.where(longer(length, (kk, 256)), 0, q - q % 256)
+        bias[at:at + kk, :] = jnp.where((key <= q) & (key >= first), 0.0, -1e30)
+        at += kk
+
+
+def table_rows(COS, SIN, length, j):
+    far = longer(length, (128, 128))
+    near = lax.rem(j, 2)
+    return (jnp.where(far, COS[rows(j), :], COS[rows(near), :]), jnp.where(far, SIN[rows(j), :], SIN[rows(near), :]))
+
+
+def matrix(W, cols):
+    w = W[:, :, :, :, cols]
+    return w.reshape(768, w.shape[-1])
+
+
+def forward_kernel(cols, qkv, out, up, down, vec, xin, cin, COS, SIN, mix,
+                   oX, oacts, oQ, oK, oV, oatt, olse, oWQ, oWO, oblock, ogmid, ogup, ogdown, ogain, vgrad,
+                   f_own, f_sib, block_w, WQ, WO, WU, WD, VEC, X, C, NB, SB,
+                   acts, Q, K, V, att, lse, middle, bias, VT, act, slope, block, ga, acts2, actsT, dg, gup, gdown, gmid,
+                   vq, vg, vu,
+                   psend, precv, lsem, gsend, grecv, asend, arecv, nsend, nrecv, fsend, frecv, xsem, csem):
+    pos = z, y, x, k = where_am_i()
+    sib = dev(z, y, x, 1 - k)
+    greet(z, y, x, k)
+    s = 2 * z + y
+    own_s = lax.rem(y + z, 2)
+    def neighbour(a, src):
+        cps = []
+        for i in range(2):
+            hi = src.at[i, pl.ds(pl.multiple_of((1 - y) * 128, 128), 128)]
+            cp = remote(hi, NB.at[a, i], nsend.at[a, i], nrecv.at[a, i], dev(z, 1 - y, x, k))
+            cp.start()
+            cps.append(cp)
+        return cps
+
+    tokens = []
+    def along_z(a, i, n, ref, dst, core):
+        g = 2 * k + i
+        me = (g == z) & (core == k)
+        cp = remote(ref, dst, asend.at[a, i, n], arecv.at[a, z], dev(g, y, x, core))
+        @pl.when(me)
+        def _():
+            pltpu.make_async_copy(ref, dst, arecv.at[a, z]).start()
+        @pl.when(jnp.logical_not(me))
+        def _():
+            cp.start()
+        tokens.append((cp, jnp.logical_not(me)))
+
+    def straight(a, src, dst):
+        for i in range(2):
+            along_z(a, i, 0, src.at[i, pl.ds(pl.multiple_of(y * 128, 128), 128)], dst(s), own_s)
+
+    def crossed(a, src, dst, cps):
+        for i in range(2):
+            cps[i].wait_recv()
+            mine = src[i, pl.ds(pl.multiple_of((1 - y) * 128, 128), 128), :]
+            far = longer(lane(vec[...], 0, 64 + i), (128, 768))
+            SB[a, i] = jnp.where(far, NB[a, i].astype(F32), mine.astype(F32)).astype(BF)
+            along_z(a, i, 1, SB.at[a, i], dst(s + 1 - 2 * y), 1 - own_s)
+
+    def arrived(a, dst, i):
+        remote(dst, dst, asend.at[a, 0, 0], arecv.at[a, i], sib).wait_recv()
+
+    to_x = lambda j: X.at[j]
+    to_c = lambda j: C.at[j // 2]
+    nx = neighbour(0, xin)
+    at, offs = 0, []
+    for n, ref in zip(cols, (qkv, out, up)):
+        half = n // 2
+        f_own[0, :, at:at + half] = ref[:, :half].astype(F32)
+        f_own[1, :, at:at + half] = ref[:, half:].astype(F32)
+        offs.append((at, half))
+        at += half
+    pre = remote(f_own.at[1 - k], f_sib, psend, precv, sib)
+    pre.start()
+    straight(0, xin, to_x)
+    lcs = [pltpu.make_async_copy(down, WD.at[z, y, x, k], lsem.at[3]), pltpu.make_async_copy(vec, VEC.at[z, y, x, k], lsem.at[4])]
+    for c in lcs: c.start()
+    pre.wait_recv()
+    for i, ((at, half), W) in enumerate(zip(offs, (WQ, WO, WU))):
+        mine = f_own[k, :, at:at + half]
+        theirs = f_sib[:, at:at + half]
+        block_w[:, at:at + half] = jnp.concatenate([jnp.where(k == 0, mine, theirs), jnp.where(k == 0, theirs, mine)], axis=0).astype(BF)
+        c = pltpu.make_async_copy(block_w.at[:, at:at + half], W.at[z, y, x, :, pl.ds(pl.multiple_of(k * half, 128), half)], lsem.at[i])
+        c.start(); lcs.append(c)
+
+    def colpart(W, half):
+        return lambda zz, yy, xx, kk: W.at[zz, yy, xx, :, pl.ds(pl.multiple_of(kk * half, 128), half)]
+    def rowpart(W):
+        return lambda zz, yy, xx, kk: W.at[zz, yy, xx, kk]
+    for c in lcs: c.wait()
+    G = [Gather(p, gsend.at[i], grecv.at[i], pos) for i, p in enumerate(
+        [rowpart(VEC), colpart(WQ, offs[0][1]), colpart(WO, offs[1][1]), colpart(WU, offs[2][1]), rowpart(WD)])]
+    gv, gq, go, gu, gd = G
+    gv.stage(0); gq.stage(0)
+    crossed(0, xin, to_x, nx)
+    nc = neighbour(1, cin)
+    gv.stage(1); gq.stage(1)
+    gv.stage(2)
+    go.stage(0)
+    fw = []
+    def forward_x(i):
+        j = own_block(jnp.int32(i), k)
+        arrived(0, X.at[j], i)
+        cp = remote(X.at[j], X.at[j], fsend.at[i], frecv.at[i], sib)
+        cp.start(); fw.append(cp)
+    gv.stage(3)
+    gq.stage(2)
+    gv.stage(4); gv.stage(5)
+    gu.stage(0)
+    for i in range(4): forward_x(i)
+    tiles = VEC[...].reshape(32, 8, 128)
+    at = 0
+    length = lane(VEC[0, 0, x, z // 2], 0, 64 + lax.rem(z, 2))
+    vq[...] = widen(tiles, 2, 72)
+    vu[...] = widen(tiles, 6, 96)
+    for n, r in enumerate((0, 1, 3, 4, 5, 7)):
+        vg[n:n + 1, :] = widen(tiles, r, 24)
+    a_gain, a_shift, bout, m_gain, m_shift, bdown = (vg[n:n + 1, :] for n in range(6))
+    bias_rows(bias, length, k)
+    go.stage(1)
+    gq.stage(3)
+    gq.stage(4)
+    straight(1, cin, to_c)
+    crossed(1, cin, to_c, nc)
+    for i in range(4): fw[i].wait_recv()
+    for j in range(8):
+        n, _ = norm(X[j].astype(F32))
+        acts[j * 128:(j + 1) * 128, :] = (n * a_gain + a_shift).astype(BF)
+    gq.stage(5)
+    go.stage(2)
+    gu.stage(1)
+    gd.stage(0)
+    exports = []
+    def export(ref, dst):
+        c = pltpu.make_async_copy(ref, dst, xsem.at[len(exports)])
+        c.start(); exports.append(c)
+
+    def keys(j):
+        a = acts[rows(j), :]
+        c, sn = table_rows(COS, SIN, length, j)
+        for t in range(3):
+            u2 = nn(a, matrix(WQ, slice(768 + t * 256, 1024 + t * 256))) + vq[:, 768 + t * 256:1024 + t * 256]
+            for h in range(2):
+                u = u2[:, h * 128:(h + 1) * 128]
+                K[rows(j), t * 256 + h * 128:t * 256 + (h + 1) * 128] = (u * c + swap(u) * sn).astype(BF)
+        V[rows(j), :] = (nn(a, matrix(WQ, slice(1536, 2304))) + vq[:, 1536:]).astype(BF)
+
+    pl.loop(0, 4)(keys)
+    go.stage(3); gu.stage(2)
+    pl.loop(4, 8)(keys)
+    go.stage(4)
+
+    @pl.loop(0, 4)
+    def _(i):
+        j = own_block(i, k)
+        a = acts[rows(j), :]
+        c, sn = table_rows(COS, SIN, length, j)
+        for t in range(3):
+            u2 = nn(a, matrix(WQ, slice(t * 256, 256 + t * 256))) + vq[:, t * 256:256 + t * 256]
+            for h in range(2):
+                u = u2[:, h * 128:(h + 1) * 128]
+                Q[rows(i), t * 256 + h * 128:t * 256 + (h + 1) * 128] = (u * c + swap(u) * sn).astype(BF) * jnp.asarray(0.125, BF)
+    gu.stage(3)
+    gd.stage(1)
+    export(X, oX); export(acts, oacts); export(Q, oQ); export(K, oK); export(V, oV)
+    export(WQ, oWQ)
+
+    def heads(h):
+        lanes = rows(h)
+        VT[...] = V[:, lanes].T
+        at = 0
+        for i in range(4):
+            kk = 256 * (i + 1)
+            qb = spread(Q[i * 128:(i + 1) * 128, lanes])
+            st = nt(K[0:kk, lanes], qb) + bias[at:at + kk, :]
+            top = jnp.max(st, axis=0, keepdims=True)
+            p = jnp.exp(st - top)
+            den = jnp.sum(p, axis=0, keepdims=True)
+            o = nn(VT[:, 0:kk], p.astype(BF)) * (1.0 / den)
+            att[i * 128:(i + 1) * 128, lanes] = pick(o)
+            lse[h, i:i + 1, :] = top + jnp.log(den)
+            at += kk
+
+    pl.loop(0, 2)(heads)
+    gu.stage(4); go.stage(5)
+    export(WO, oWO)
+    pl.loop(2, 4)(heads)
+    gd.stage(2)
+    pl.loop(4, 6)(heads)
+    gd.stage(3)
+    export(att, oatt); export(lse, olse)
+
+    @pl.loop(0, 4)
+    def _(i):
+        j = own_block(i, k)
+        middle[rows(i), :] = X[j].astype(F32) + (nn(att[rows(i), :].astype(BF), WO[...].reshape(768, 768)) + bout)
+    m5 = mix[5]
+    for i in range(4):
+        arrived(1, C.at[i], i)
+        r = slice(i * 128, (i + 1) * 128)
+        mid = middle[r, :]
+        n, _ = norm(mid)
+        a2 = (n * m_gain + m_shift).astype(BF)
+        acts2[r, :] = a2
+        actsT[:, r] = a2.T
+        dg[r, :] = (m5 * C[i].astype(F32)).astype(BF)
+        block[r, :] = mid + bdown
+        ga[r, :] = jnp.zeros_like(mid)
+    gu.stage(5)
+    gd.stage(4)
+    vgrad[...] = jnp.zeros_like(vgrad)
+
+    def put_vec(row, v):
+        for t in range(v.shape[1] // 128):
+            vgrad[row + t:row + t + 1, :] = v[:, t * 128:(t + 1) * 128]
+    put_vec(72, jnp.sum(dg[...].astype(F32), axis=0, keepdims=True))
+
+    @pl.loop(0, 8)
+    def _(f):
+        c = rows(f, 384)
+        u = nn(acts2[...], matrix(WU, c)) + vu[:, c]
+        half_erf = 0.5 * lax.erf(u * (2.0 ** -0.5)) + 0.5
+        slope[:, c] = half_erf + u * (jnp.exp(u * u * -0.5) * (1.0 / math.sqrt(2 * math.pi)))
+        act[:, c] = (u * half_erf).astype(BF)
+    gd.stage(5)
+
+    @pl.loop(0, 4)
+    def _(f):
+        c = rows(f, 768)
+        wd = WD[f].reshape(768, 768)
+        a = act[:, c]
+        block[...] += nn(a, wd)
+        upg = (nt(dg[...], wd) * slope[:, c]).astype(BF)
+        g = jnp.sum(upg.astype(F32), axis=0, keepdims=True)
+        for t in range(6):
+            vgrad[pl.ds(48 + f * 6 + t, 1), :] = g[:, t * 128:(t + 1) * 128]
+        gdown[c, :] = nn(a.T, dg[...]).astype(BF)
+        pltpu.make_async_copy(gdown.at[c, :], ogdown.at[c, :], csem.at[0, f]).start()
+        gup[:, c] = nn(actsT[...], upg).astype(BF)
+        pltpu.make_async_copy(gup.at[:, c], ogup.at[:, c], csem.at[1, f]).start()
+        ga[...] += nt(upg, matrix(WU, c))
+
+    total = jnp.zeros((1, 768), F32)
+    gg = jnp.zeros((1, 768), F32)
+    gs = jnp.zeros((1, 768), F32)
+    for i in range(4):
+        r = slice(i * 128, (i + 1) * 128)
+        n, inv = norm(middle[r, :])
+        e = ga[r, :]
+        cf = C[i].astype(F32)
+        gg += jnp.sum(e * n, axis=0, keepdims=True)
+        gs += jnp.sum(e, axis=0, keepdims=True)
+        gmid[r, :] = m5 * cf + norm_grad(e, n, inv, m_gain)
+        total += jnp.sum(cf * block[r, :], axis=0, keepdims=True)
+    put_vec(36, gg); put_vec(42, gs)
+    ogain[...] = jnp.broadcast_to(a_gain, (8, 768))
+    whole = jnp.sum(total, axis=1, keepdims=True)
+    vgrad[78:79, :] = jnp.where(lax.broadcasted_iota(jnp.int32, (1, 128), 1) == 5, jnp.broadcast_to(whole, (1, 128)), 0.0)
+    vgrad[79:80, :] = jnp.broadcast_to(length, (1, 128))
+    export(gmid, ogmid); export(block, oblock)
+    for f in range(4):
+        c = slice(f * 768, (f + 1) * 768)
+        pltpu.make_async_copy(gdown.at[c, :], ogdown.at[c, :], csem.at[0, f]).wait()
+        pltpu.make_async_copy(gup.at[:, c], ogup.at[:, c], csem.at[1, f]).wait()
+    for c in exports: c.wait()
+    for c in fw + nx + nc: c.wait_send()
+    for cp, cond in tokens:
+        @pl.when(cond)
+        def _():
+            cp.wait_send()
+    pre.wait_send()
+
+
+def forward_call(qkv, out, up, down, vec, xin, cin, COS, SIN, mix):
+    cols = (qkv.shape[1], out.shape[1], up.shape[1])
+    H = sum(cols) // 2
+    any_ = pl.BlockSpec(memory_space=pl.ANY)
+    T = lambda n, t=BF: ((n, 768), t)
+    shapes = [((8, 128, 768), BF), T(1024), T(512), T(1024), T(1024), T(512, F32), ((6, 4, 256), F32),
+              ((4, 2, 2, 48, 2304), BF), ((4, 2, 2, 48, 768), BF), T(512, F32), T(512, F32), ((768, 3072), BF), T(3072)]
+    DS = pltpu.SemaphoreType.DMA
+    return pl.pallas_call(functools.partial(forward_kernel, cols),
+        out_shape=[sd(*t) for t in shapes] + [sd((8, 768), F32), sd((80, 128), F32)],
+        in_specs=[vs] * 9 + [ss], out_specs=[any_] * len(shapes) + [vs, vs],
+        scratch_shapes=[VM((2, 24, H), F32), VM((24, H), F32), VM((48, H), BF),
+                        VM((4, 2, 2, 48, 2304), BF), VM((4, 2, 2, 48, 768), BF), VM((4, 2, 2, 48, 3072), BF), VM((4, 2, 2, 2, 96, 768), BF),
+                        VM((4, 2, 2, 2, 8, 128), F32), VM((8, 128, 768), BF), VM((4, 128, 768), BF), VM((2, 2, 128, 768), BF), VM((2, 2, 128, 768), BF),
+                        VM((1024, 768), BF), VM((512, 768), BF), VM((1024, 768), BF), VM((1024, 768), BF), VM((512, 768), F32),
+                        VM((6, 4, 256), F32), VM((512, 768), F32), VM((2560, 256), F32), VM((128, 1024), BF),
+                        VM((512, 3072), BF), VM((512, 3072), F32), VM((512, 768), F32), VM((512, 768), F32), VM((512, 768), BF),
+                        VM((768, 512), BF), VM((512, 768), BF), VM((768, 3072), BF), VM((3072, 768), BF), VM((512, 768), F32),
+                        VM((1, 2304), F32), VM((8, 768), F32), VM((1, 3072), F32),
+                        DS, DS, DS((5,)), DS((5, 10)), DS((5, 10)), DS((2, 2, 2)), DS((2, 4)), DS((2, 2)), DS((2, 2)), DS((4,)), DS((4,)),
+                        DS((12,)), DS((2, 4))],
+        compiler_params=pltpu.CompilerParams(collective_id=0, has_side_effects=True, vmem_limit_bytes=63 * 2**20),
+    )(qkv, out, up, down, vec, xin, cin, COS, SIN, mix)
 
 
 class Scatter:
@@ -1112,7 +1444,7 @@
             for c in [self.pre, self.b0, self.b1, self.c] + self.zs: c.wait_send()
 
 
-def reduce_kernel(cols, flag, gqkv, gout, gup, gdown, e, gmid, block, XM, XA, gain, vin,
+def reduce_kernel(cols, flag, gqkv, gout, gup, gdown, e, gmid, block, X, gain, vin,
                   oq, oo, ou, od, vout, H0, HL, HS,
                   PQ, AQ, BQ, CQ, ZQ, PO, AO, BO, CO, ZO, PU, AU, BU, CU, ZU, PD, AD, BD, CD, ZD,
                   fin, fsib, es, er, gx, bl, vbuf, vrec,
@@ -1177,8 +1509,7 @@
         gsh = jnp.zeros((1, 768), F32)
         for i in range(4):
             j = own_block(jnp.int32(i), k)
-            alt = jnp.logical_and(jnp.logical_not(is_long), lax.rem(j, 2) != y)
-            n, inv = norm(jnp.where(alt, XA[i], XM[j]).astype(F32))
+            n, inv = norm(X[j].astype(F32))
             ee = e[rows(j), :] + er[i].astype(F32)
             gg += jnp.sum(ee * n, axis=0, keepdims=True)
             gsh += jnp.sum(ee, axis=0, keepdims=True)
@@ -1261,32 +1592,20 @@
     seq, batch = lax.axis_index("seq"), lax.axis_index("batch")
     z, y, x, k = seq // 2, seq % 2, batch // 2, batch % 2
     vectors = (attn_gain, attn_shift, qkv_bias, out_bias, mlp_gain, mlp_shift, up_bias, down_bias)
-    packed = jnp.concatenate([v.astype(F32) for v in vectors] + [seq_lengths.astype(F32)])
-    packed = jnp.pad(packed, (0, 1024 - packed.shape[0])).reshape(8, 128)
-    QKV, OUT, UP, DOWN, VEC, XM, XA, CM, CA = gather_call(qkv_weight, out_weight, up_weight, down_weight, packed, inputs, cotangent)
-    wqkv, wout, wup = (w.reshape(768, w.shape[-1]) for w in (QKV, OUT, UP))
-    wdown = DOWN.reshape(3072, 768)
-    flat = VEC.reshape(32, 1024)
-    full, at = [], 0
-    for v in vectors:
-        n = v.shape[0]
-        full.append(flat[:, at:at + n].reshape(1, 32 * n))
-        at += n
-    a_gain, a_shift, bqkv, bout, m_gain, m_shift, bup, bdown = full
-    length = VEC[0, 0, :, :, 0, :].reshape(2, 2, 0 + 128)[:, :, 0] if False else flat[:4, at:at + 2].reshape(2, 4)
-    lens = lax.dynamic_index_in_dim(length, x, 0, keepdims=False)
-    flag = (lax.dynamic_index_in_dim(lens, z, 0, keepdims=True) == LONG_LEN).astype(jnp.int32)
+    lens = seq_lengths.astype(F32)
+    packed = jnp.stack([jnp.pad(v.astype(F32), (0, 128 - v.shape[0])) for v in vectors])
+    packed = packed.at[0, 64:66].set(lens)
     COS, SIN = (jnp.asarray(t) for t in rope_tables())
-    acts, Q, K, V, att, lse, middle = attn_fwd_call(flag, XM, XA, wqkv, wout, a_gain, a_shift, bqkv, bout, COS, SIN)
-    block, gmid, gup, gdown, g_mgain, g_mshift, g_bup, g_bdown, mixsum = mlp_call(
-        flag, mix_weights, middle, CM, CA, wup, wdown, m_gain, m_shift, bup, bdown)
-    e, gqkv, gout, g_bqkv, g_bout = attn_bwd_call(flag, gmid, XM, XA, acts, Q, K, V, att, lse, wqkv, wout, a_gain, COS, SIN)
+    X, acts, Q, K, V, att, lse, WQ, WO, block, gmid, gup, gdown, gain, vgrad = forward_call(
+        qkv_weight, out_weight, up_weight, down_weight, packed, inputs, cotangent, COS, SIN, mix_weights)
+    wqkv, wout, a_gain = WQ.reshape(768, 2304), WO.reshape(768, 768), gain[:1]
+    flag = (vgrad[79, :1] == LONG_LEN).astype(jnp.int32)
+    e, gqkv, gout, g_bqkv, g_bout = attn_bwd_call(flag, gmid, acts, Q, K, V, att, lse, wqkv, wout, COS, SIN)
     earlier, cot = history.astype(F32), cotangent.astype(F32)
-    mix_terms = jnp.concatenate([jnp.sum(earlier * cot[None], axis=(1, 2, 3)), jnp.sum(mixsum)[None]])
+    mix_terms = jnp.sum(earlier * cot[None], axis=(1, 2, 3))
     grad_history = (mix_weights[:-1, None, None, None] * cot[None]).astype(BF)
-    vin = jnp.concatenate([jnp.zeros((1536,), F32)] + [v.reshape(-1) for v in (g_bqkv, g_bout, g_mgain, g_mshift, g_bup, g_bdown)]
-                          + [mix_terms, jnp.zeros((250,), F32)]).reshape(80, 128)
-    oq, oo, ou, od, vout, H0, HL, HS = reduce_call(flag, gqkv, gout, gup, gdown, e, gmid, block, XM, XA, a_gain, vin)
+    vin = vgrad.at[12:30].set(g_bqkv.reshape(18, 128)).at[30:36].set(g_bout.reshape(6, 128)).at[78, :5].set(mix_terms)
+    oq, oo, ou, od, vout, H0, HL, HS = reduce_call(flag, gqkv, gout, gup, gdown, e, gmid, block, X, a_gain, vin)
     is_long = (seq_lengths == LONG_LEN)[None, :, None, None]
     other = jnp.where(is_long, HL, HS)
     home = jnp.where(y == 0, jnp.concatenate([H0, other], axis=2), jnp.concatenate([other, H0], axis=2))

time: 399 us -> 326 us (0.82)
  Pallas kernels: 343 us -> 285 us
  local copies, waits for them, and re-layouts: 39.7 us -> 21.4 us
    pallas_call x3 -> x1, Pallas kernels: 188 us -> 134 us  [forward_call(): pl.pallas_call(functools.partial(forward_kernel, cols), out_shape=[sd(*t)...]
    unnamed x57 -> x20, local copies, waits for them, and re-layouts: 19.9 us -> 3.36 us
    concatenate x2 -> x0, local copies, waits for them, and re-layouts: 6.76 us -> none  [the longest x1 5.42 us: fast_shards(): jnp.concatenate([v.astype(F32) for v in vectors] + [seq_lengths.astype(F3...]
    scatter x0 -> x4, local copies, waits for them, and re-layouts: none -> 5.56 us  [the longest x3 3.99 us: fast_shards(): vgrad.at[12:30].set(g_bqkv.reshape(18, 128)).at[30:36]]
    reshape x10 -> x0, local copies, waits for them, and re-layouts: 5.54 us -> none  [the longest x8 5.45 us: fast_shards(): full.append(flat[:, at:at + n].reshape(1, 32 * n))]
where the time goes in v2:
time: 326 us; the launch traced here: 325 us
  Pallas kernels  285 us (87%)
  local copies, waits for them, and re-layouts  21.4 us (7%)
  other arithmetic  16.4 us (5%)
    pallas_call x1, Pallas kernels, forward_call(): pl.pallas_call(functools.partial(forward_kernel, cols), out_shape=[sd(*t)...  134 us
    pallas_call x1, Pallas kernels, reduce_call(): pl.pallas_call(functools.partial(reduce_kernel, cols), out_shape=[sd((24,...  112 us
    pallas_call x1, Pallas kernels, attn_bwd_call(): pl.pallas_call(attn_bwd, out_shape=[sd((1024, 768), F32), sd((768, 2304),...  39.7 us

profile of v2, /device:TPU:0, one launch (start us, length us, event | category | flops | bytes accessed | tf_op | source)
XLA Modules:
  0.0 324.6 jit_solution(18292897492236132395)
XLA Ops:
  0.6 0.7 pad_bitcast_fusion
  1.3 0.7 pad_bitcast_fusion.2
  2.0 0.7 pad_bitcast_fusion.4
  2.7 0.7 pad_bitcast_fusion.6
  3.4 0.6 fusion.4
  4.0 1.3 and_reduce_fusion
  5.3 2.7 broadcast_select_fusion.1
  8.0 1.6 scatter.14.vec
  9.5 0.6 copy-done.5
  10.1 133.9 %shard_map.306 = (bf16[8,128,768]{2,1,0:T(8,128)(2,1)}, bf16[1024,768]{1,0:T(8,128)(2,1)}, bf16[512,768]{1,0:T(8,128)(2,1)}, bf16[1024,768]{1,0:T(8,128)(2,1)}, ...) custom-call(bf16[24,2304]{1,0:T(8,128)(2,1)} %qkv.1, ...), custom_call_target="tpu_custom_call" | custom-call | tf_op jit(solution)/shard_map/pallas_call | solution.py:1367
  144.0 1.2 slice.101
  145.9 39.7 %shard_map.307 = (f32[1024,768]{1,0:T(8,128)}, bf16[768,2304]{1,0:T(8,128)(2,1)}, bf16[768,768]{1,0:T(8,128)(2,1)}, f32[1,2304]{1,0:T(1,128)}, f32[1,768]{1,0:T(1,128)}) custom-call(s32[1]{0:T(128)} %bitcast.12.flag, f32[512,768]{1,0:T(8,128)} %get-tuple-element.93.gmid, bf16[1024,768]{1,0:T(8,128)(2,1)} %get-tuple-element.94.acts, ...), custom_call_target="tpu_custom_call" | custom-call | tf_op jit(solution)/shard_map/pallas_call | solution.py:1044
  185.6 0.7 reduce.13
  186.3 1.4 scatter.15
  187.7 0.7 reduce.14
  188.4 1.3 scatter.16
  189.8 5.6 %fusion.1 = (f32[5]{0:T(128)S(1)}, f32[2,256,768]{2,1,0:T(8,128)S(1)}, bf16[5,2,256,768]{3,2,1,0:T(8,128)(2,1)}) fusion(bf16[5,2,256,768]{3,2,1,0:T(8,128)(2,1)} %param.28, f32[2,256,768]{2,1,0:T(8,128)S(1)} %convert_element_type.47, f32[5]{0:T(128)S(1)} %bitcast.47), kind=kLoop, calls=%fused_computation.3 | loop fusion | flops 13369339 | bytes 11010088 | tf_op jit(solution)/shard_map/reduce_sum | solution.py:1605
  195.5 1.3 scatter.19.vin
  196.8 1.3 slice.102.gain
  198.1 111.8 %shard_map.308 = (f32[24,2304]{1,0:T(8,128)}, f32[24,768]{1,0:T(8,128)}, f32[24,3072]{1,0:T(8,128)}, f32[96,768]{1,0:T(8,128)}, f32[80,128]{1,0:T(8,128)}, /*ind...) custom-call(s32[1]{0:T(128)} %bitcast.12.flag, ...), custom_call_target="tpu_custom_call" | custom-call | tf_op jit(solution)/shard_map/pallas_call | solution.py:1581
  310.0 1.5 broadcast_select_fusion
  311.5 2.0 maximum_select_fusion
  314.0 1.7 fusion.2
  315.8 0.9 slice_bitcast_fusion
  316.7 1.4 fusion.3
  318.1 1.3 dynamic_slice.26
  319.4 1.3 dynamic_slice.30
  320.7 1.2 slice.108
  321.9 0.7 copy.43
  322.5 0.6 copy.44
  323.2 0.7 copy.45
  323.9 0.7 copy.46
  (21 shorter events, 0.8 us)
Async XLA Ops:
  9.5 0.6 copy-start.5
  145.8 43.9 %copy-start = (bf16[2,256,768]{2,1,0:T(8,128)(2,1)S(1)}, bf16[2,256,768]{2,1,0:T(8,128)(2,1)}, u32[]{:S(2)}) copy-start(bf16[2,256,768]{2,1,0:T(8,128)(2,1)} %cin.1) | copy-start | bytes 2359300
  185.6 4.3 %copy-start.6 = (f32[6]{0:T(128)S(1)}, f32[6]{0:T(128)}, u32[]{:S(2)}) copy-start(f32[6]{0:T(128)} %mix.1) | copy-start | bytes 76
  198.1 111.9 %copy-start.7 = (s32[2]{0:T(128)S(1)}, s32[2]{0:T(128)}, u32[]{:S(2)}) copy-start(s32[2]{0:T(128)} %param.29) | copy-start | bytes 28
  315.8 6.1 %copy-start.3 = (f32[24,2304]{1,0:T(8,128)S(1)}, f32[24,2304]{1,0:T(8,128)}, u32[]{:S(2)}) copy-start(f32[24,2304]{1,0:T(8,128)} %get-tuple-element.160) | copy-start | bytes 663556
  315.8 6.8 %copy-start.4 = (f32[24,768]{1,0:T(8,128)S(1)}, f32[24,768]{1,0:T(8,128)}, u32[]{:S(2)}) copy-start(f32[24,768]{1,0:T(8,128)} %get-tuple-element.162) | copy-start | bytes 221188
  315.8 7.4 %copy-start.2 = (f32[24,3072]{1,0:T(8,128)S(1)}, f32[24,3072]{1,0:T(8,128)}, u32[]{:S(2)}) copy-start(f32[24,3072]{1,0:T(8,128)} %get-tuple-element.166) | copy-start | bytes 884740
  315.8 8.1 %copy-start.1 = (f32[96,768]{1,0:T(8,128)S(1)}, f32[96,768]{1,0:T(8,128)}, u32[]{:S(2)}) copy-start(f32[96,768]{1,0:T(8,128)} %get-tuple-element.168) | copy-start | bytes 884740

commit v3 on v2

--- a/solution.py
+++ b/solution.py
@@ -1100,7 +1100,7 @@
 def forward_kernel(cols, qkv, out, up, down, vec, xin, cin, COS, SIN, mix,
                    oX, oacts, oQ, oK, oV, oatt, olse, oWQ, oWO, oblock, ogmid, ogup, ogdown, ogain, vgrad,
                    f_own, f_sib, block_w, WQ, WO, WU, WD, VEC, X, C, NB, SB,
-                   acts, Q, K, V, att, lse, middle, bias, VT, act, slope, block, ga, acts2, actsT, dg, gup, gdown, gmid,
+                   acts, Q, K, V, att, lse, middle, bias, VT, act, slope, block, ga, acts2, actsT, dg, gup, gdown, a1T, bl,
                    vq, vg, vu,
                    psend, precv, lsem, gsend, grecv, asend, arecv, nsend, nrecv, fsend, frecv, xsem, csem):
     pos = z, y, x, k = where_am_i()
@@ -1247,7 +1247,12 @@
                 Q[rows(i), t * 256 + h * 128:t * 256 + (h + 1) * 128] = (u * c + swap(u) * sn).astype(BF) * jnp.asarray(0.125, BF)
     gu.stage(3)
     gd.stage(1)
-    export(X, oX); export(acts, oacts); export(Q, oQ); export(K, oK); export(V, oV)
+    for i in range(4):
+        j = own_block(jnp.int32(i), k)
+        export(X.at[j], oX.at[i])
+    for j in range(8):
+        a1T[:, j * 128:(j + 1) * 128] = acts[j * 128:(j + 1) * 128, :].T
+    export(a1T, oacts); export(Q, oQ); export(K, oK); export(V, oV)
     export(WQ, oWQ)
 
     def heads(h):
@@ -1335,14 +1340,15 @@
         cf = C[i].astype(F32)
         gg += jnp.sum(e * n, axis=0, keepdims=True)
         gs += jnp.sum(e, axis=0, keepdims=True)
-        gmid[r, :] = m5 * cf + norm_grad(e, n, inv, m_gain)
+        ga[r, :] = m5 * cf + norm_grad(e, n, inv, m_gain)
         total += jnp.sum(cf * block[r, :], axis=0, keepdims=True)
+        bl[i] = block[r, :].astype(BF)
     put_vec(36, gg); put_vec(42, gs)
     ogain[...] = jnp.broadcast_to(a_gain, (8, 768))
     whole = jnp.sum(total, axis=1, keepdims=True)
     vgrad[78:79, :] = jnp.where(lax.broadcasted_iota(jnp.int32, (1, 128), 1) == 5, jnp.broadcast_to(whole, (1, 128)), 0.0)
     vgrad[79:80, :] = jnp.broadcast_to(length, (1, 128))
-    export(gmid, ogmid); export(block, oblock)
+    export(ga, ogmid); export(bl, oblock)
     for f in range(4):
         c = slice(f * 768, (f + 1) * 768)
         pltpu.make_async_copy(gdown.at[c, :], ogdown.at[c, :], csem.at[0, f]).wait()
@@ -1361,8 +1367,8 @@
     H = sum(cols) // 2
     any_ = pl.BlockSpec(memory_space=pl.ANY)
     T = lambda n, t=BF: ((n, 768), t)
-    shapes = [((8, 128, 768), BF), T(1024), T(512), T(1024), T(1024), T(512, F32), ((6, 4, 256), F32),
-              ((4, 2, 2, 48, 2304), BF), ((4, 2, 2, 48, 768), BF), T(512, F32), T(512, F32), ((768, 3072), BF), T(3072)]
+    shapes = [((4, 128, 768), BF), ((768, 1024), BF), T(512), T(1024), T(1024), T(512, F32), ((6, 4, 256), F32),
+              ((4, 2, 2, 48, 2304), BF), ((4, 2, 2, 48, 768), BF), ((4, 128, 768), BF), T(512, F32), ((768, 3072), BF), T(3072)]
     DS = pltpu.SemaphoreType.DMA
     return pl.pallas_call(functools.partial(forward_kernel, cols),
         out_shape=[sd(*t) for t in shapes] + [sd((8, 768), F32), sd((80, 128), F32)],
@@ -1373,52 +1379,51 @@
                         VM((1024, 768), BF), VM((512, 768), BF), VM((1024, 768), BF), VM((1024, 768), BF), VM((512, 768), F32),
                         VM((6, 4, 256), F32), VM((512, 768), F32), VM((2560, 256), F32), VM((128, 1024), BF),
                         VM((512, 3072), BF), VM((512, 3072), F32), VM((512, 768), F32), VM((512, 768), F32), VM((512, 768), BF),
-                        VM((768, 512), BF), VM((512, 768), BF), VM((768, 3072), BF), VM((3072, 768), BF), VM((512, 768), F32),
+                        VM((768, 512), BF), VM((512, 768), BF), VM((768, 3072), BF), VM((3072, 768), BF), VM((768, 1024), BF), VM((4, 128, 768), BF),
                         VM((1, 2304), F32), VM((8, 768), F32), VM((1, 3072), F32),
                         DS, DS, DS((5,)), DS((5, 10)), DS((5, 10)), DS((2, 2, 2)), DS((2, 4)), DS((2, 2)), DS((2, 2)), DS((4,)), DS((4,)),
-                        DS((12,)), DS((2, 4))],
+                        DS((16,)), DS((2, 4))],
         compiler_params=pltpu.CompilerParams(collective_id=0, has_side_effects=True, vmem_limit_bytes=63 * 2**20),
     )(qkv, out, up, down, vec, xin, cin, COS, SIN, mix)
 
 
 class Scatter:
-    STAGES = 5
-
-    def __init__(self, part, PA, RA, RB, RC, RZ, put, send, recv, pos):
-        self.__dict__.update(locals())
+    STAGES = 6
+
+    def __init__(self, mine, theirs, RA, RB, RC, RZ, put, finish, send, recv, pos, load=None):
+        self.mine, self.RA, self.RB, self.RC, self.RZ, self.put, self.finish, self.pos, self.load = mine, RA, RB, RC, RZ, put, finish, pos, load
         z, y, x, k = pos
         self.own = (y, x)
         self.p2 = jnp.where(k == 0, 1 - y, y), jnp.where(k == 0, x, 1 - x)
         self.p3 = jnp.where(k == 0, y, 1 - y), jnp.where(k == 0, 1 - x, x)
         self.d4 = 1 - y, 1 - x
-        blk = lambda yx: PA.at[:, yx[0], yx[1]]
+        blk = lambda yx: mine(slice(None), yx[0], yx[1])
         n3, n2 = dev(z, *self.p3, k), dev(z, *self.p2, k)
-        self.pre = remote(part(slice(None), slice(None), slice(None), 1 - k), RA, send.at[0], recv.at[0], dev(z, y, x, 1 - k))
+        self.pre = remote(theirs, RA, send.at[0], recv.at[0], dev(z, y, x, 1 - k))
         self.b1 = remote(blk(self.d4), RB.at[1], send.at[1], recv.at[1], n3)
         self.b0 = remote(blk(self.p3), RB.at[0], send.at[2], recv.at[2], n3)
         self.c = remote(blk(self.p2), RC, send.at[3], recv.at[3], n2)
-        self.zs = [remote(PA.at[lax.rem(z + d, 4), y, x], RZ.at[d - 1], send.at[3 + d], recv.at[3 + d],
+        self.zs = [remote(mine(lax.rem(z + d, 4), y, x), RZ.at[d - 1], send.at[3 + d], recv.at[3 + d],
                           dev(lax.rem(z + d, 4), y, x, k)) for d in (1, 2, 3)]
+        self.sends = [self.pre, self.b1, self.b0, self.c] + self.zs
 
     def add(self, yx, other):
         @pl.loop(0, 4)
         def _(i):
-            a = self.PA[i, yx[0], yx[1]].astype(F32) + other[i].astype(F32)
-            self.PA[i, yx[0], yx[1]] = a.astype(BF)
+            ref = self.mine(i, yx[0], yx[1])
+            ref[...] = (ref[...].astype(F32) + other[i].astype(F32)).astype(BF)
 
     def first(self, yx):
-        k = self.pos[3]
-        @pl.loop(0, 4)
-        def _(i):
-            a = self.part(i, yx[0], yx[1], k)[...].astype(F32) + self.RA[i, yx[0], yx[1]].astype(F32)
-            self.PA[i, yx[0], yx[1]] = a.astype(BF)
+        self.add(yx, self.RA.at[:, yx[0], yx[1]])
 
     def stage(self, n):
         z, y, x, k = self.pos
         if n == 0:
+            if self.load is not None: self.load.start()
             self.pre.start()
         elif n == 1:
             self.pre.wait_recv()
+            if self.load is not None: self.load.wait()
             self.first(self.d4)
             self.b1.start()
             self.first(self.p3)
@@ -1437,61 +1442,72 @@
             for c in self.zs: c.start()
         elif n == 4:
             for c in self.zs: c.wait_recv()
-            tot = self.PA[z, y, x].astype(F32)
+            tot = self.mine(z, y, x)[...].astype(F32)
             for i in range(3):
                 tot = tot + self.RZ[i].astype(F32)
             self.put(tot)
-            for c in [self.pre, self.b0, self.b1, self.c] + self.zs: c.wait_send()
-
-
-def reduce_kernel(cols, flag, gqkv, gout, gup, gdown, e, gmid, block, X, gain, vin,
-                  oq, oo, ou, od, vout, H0, HL, HS,
-                  PQ, AQ, BQ, CQ, ZQ, PO, AO, BO, CO, ZO, PU, AU, BU, CU, ZU, PD, AD, BD, CD, ZD,
-                  fin, fsib, es, er, gx, bl, vbuf, vrec,
-                  ssem, rsem, hsend, h0, hl, hs, misc_s, misc_r, vsend, vrecv):
+        elif n == 5:
+            self.finish()
+            for c in self.sends: c.wait_send()
+
+
+def backward_kernel(gup, gdown, block, gmid, X, actsT, Q, Kin, Vin, att, lse, WQ, WO, gain, COS, SIN, vin,
+                    oq, oo, ou, od, vout, H0, HL, HS,
+                    K, V, bias, KT, da, dQ, dK, dV, agrad, actsqT, GO, GQ, PU, PD,
+                    AU, BU, CU, ZU, AD, BD, CD, ZD, AO, BO, CO, ZO, AQ, BQ, CQ, ZQ,
+                    fin, fsib, finu, fsibu, es, er, gx, vbuf, vrec,
+                    ssem, rsem, ldsem, fsend, frecv, hsend, h0, hl, hs, nsend, esem_s, esem_r, vsend, vrecv, csem):
     pos = z, y, x, k = where_am_i()
-    is_long = flag[0] != 0
+    sib = dev(z, y, x, 1 - k)
     greet(z, y, x, k)
-    sib = dev(z, y, x, 1 - k)
-    for i in range(4):
-        es[i] = e[rows(own_block(jnp.int32(i), 1 - k)), :].astype(BF)
-    ecp = remote(es, er, misc_s.at[0], misc_r.at[0], sib)
-    ecp.start()
-    halves = [c // 2 for c in cols]
-
-    def colpart(W, half):
-        def f(zz, yy, xx, kk):
-            return W.at[zz, yy, xx, :, pl.ds(pl.multiple_of(kk * half, 128), half)]
-        return f
-    offs = [0, halves[0], halves[0] + halves[1]]
-    def put_cols(i):
+    length = vin[79:80, 0:1]
+    ck = pltpu.make_async_copy(Kin, K, csem.at[0])
+    cv = pltpu.make_async_copy(Vin, V, csem.at[1])
+    ck.start(); cv.start()
+    half_of = lambda kk, half: pl.ds(pl.multiple_of(kk * half, 128), half)
+
+    def col_scatter(a, G, half, bufs, n, out, at, width, fi, fs, hbm=None):
         def put(t):
-            fin[0, :, offs[i]:offs[i] + halves[i]] = t[:24]
-            fin[1, :, offs[i]:offs[i] + halves[i]] = t[24:]
-        return put
+            fi[n, 0] = t[:24]
+            fi[n, 1] = t[24:]
+            last.start()
+        last = remote(fi.at[n, 1 - k], fs.at[n], fsend.at[a], frecv.at[a], sib)
+        def finish():
+            last.wait_recv()
+            mine, theirs = fi[n, k], fs[n]
+            out[:, at:at + half] = jnp.where(k == 0, mine, theirs)
+            out[:, at + half:at + 2 * half] = jnp.where(k == 0, theirs, mine)
+            last.wait_send()
+        if hbm is None:
+            mine = lambda zz, yy, xx: G.at[zz, yy, xx, :, half_of(k, half)]
+            theirs = G.at[:, :, :, :, half_of(1 - k, half)]
+            load = None
+        else:
+            mine = lambda zz, yy, xx: G.at[zz, yy, xx]
+            theirs = hbm.at[:, :, :, :, half_of(1 - k, half)]
+            load = pltpu.make_async_copy(hbm.at[:, :, :, :, half_of(k, half)], G, ldsem.at[a])
+        return Scatter(mine, theirs, *bufs, put, finish, ssem.at[a], rsem.at[a], pos, load)
+
     def put_down(t):
         od[...] = t
-    S = lambda a, part, bufs, put: Scatter(part, *bufs, put, ssem.at[a], rsem.at[a], pos)
-    gs = [S(0, lambda zz, yy, xx, kk: gdown.at[zz, yy, xx, kk], (PD, AD, BD, CD, ZD), put_down),
-          S(1, colpart(gup, halves[2]), (PU, AU, BU, CU, ZU), put_cols(2)),
-          S(2, colpart(gout, halves[1]), (PO, AO, BO, CO, ZO), put_cols(1)),
-          S(3, colpart(gqkv, halves[0]), (PQ, AQ, BQ, CQ, ZQ), put_cols(0))]
+    sdn = Scatter(lambda zz, yy, xx: PD.at[zz, yy, xx], gdown.at[:, :, :, 1 - k], AD, BD, CD, ZD, put_down, lambda: None,
+                  ssem.at[0], rsem.at[0], pos, pltpu.make_async_copy(gdown.at[:, :, :, k], PD, ldsem.at[0]))
+    sup = col_scatter(1, PU, 1536, (AU, BU, CU, ZU), 0, ou, 0, 3072, finu, fsibu, gup)
+    sout = col_scatter(2, GO, 384, (AO, BO, CO, ZO), 0, oo, 0, 768, fin, fsib)
+    sq, sk, sv = (col_scatter(3 + n, GQ.at[n], 384, (AQ.at[n], BQ.at[n], CQ.at[n], ZQ.at[n]), 1 + n, oq, 768 * n, 768, fin, fsib)
+                  for n in range(3))
+    sdn.stage(0); sup.stage(0)
+
     homes = []
-    g = z
     def send_home(a, buf):
+        slot = lax.rem(z, 2)
         for i in range(4):
             j = own_block(jnp.int32(i), k)
-            yj = lax.rem(j, 2)
-            zj = jnp.int32(i)
-            core = g // 2
-            straight = yj == y
-            slot = lax.rem(g, 2)
-            for n, (dst, rs, yd, cond) in enumerate((
-                (H0.at[a, slot], h0.at[a, slot], y, straight),
-                (HL.at[a, slot], hl.at[a, slot], 1 - y, jnp.logical_not(straight)),
-                (HS.at[a, slot], hs.at[a, slot], y, jnp.logical_not(straight)))):
-                me = (zj == z) & (yd == y) & (core == k)
-                cp = remote(buf.at[i], dst, hsend.at[a, i, n], rs, dev(zj, yd, x, core))
+            straight = lax.rem(j, 2) == y
+            me = (i == z) & (z // 2 == k)
+            for n, (dst, rs, cond) in enumerate(((H0.at[a, slot], h0.at[a, slot], straight),
+                                                 (HS.at[a, slot], hs.at[a, slot], jnp.logical_not(straight)))):
+                cp = remote(buf.at[i], dst, hsend.at[a, i, n], rs, dev(jnp.int32(i), y, x, z // 2))
                 @pl.when(cond & me)
                 def _():
                     pltpu.make_async_copy(buf.at[i], dst, rs).start()
@@ -1499,29 +1515,131 @@
                 def _():
                     cp.start()
                 homes.append((cp, cond & jnp.logical_not(me)))
+
+    across = []
+    def home_across(a):
+        for i in range(2):
+            remote(HS.at[a, i], HS.at[a, i], nsend.at[a, i], hs.at[a, i], sib).wait_recv()
+            cp = remote(HS.at[a, i], HL.at[a, i], nsend.at[a, i], hl.at[a, i], dev(z, 1 - y, x, k))
+            cp.start(); across.append(cp)
+
+    def home_done(a):
+        for i in range(2):
+            remote(H0.at[a, i], H0.at[a, i], nsend.at[a, i], h0.at[a, i], sib).wait_recv()
+            remote(HL.at[a, i], HL.at[a, i], nsend.at[a, i], hl.at[a, i], sib).wait_recv()
+
+    bias_rows(bias, length, k)
+    agrad[...] = gmid[...].astype(BF)
+    vbuf[0] = vin[...]
+
+    def put_vec(row, v):
+        for t in range(v.shape[1] // 128):
+            vbuf[0, row + t:row + t + 1, :] = v[:, t * 128:(t + 1) * 128]
+    put_vec(30, jnp.sum(agrad[...].astype(F32), axis=0, keepdims=True))
+    wo = lambda: WO[...].reshape(768, 768)
+
+    @pl.loop(0, 4)
+    def _(i):
+        da[rows(i), :] = nt(agrad[rows(i), :], wo()).astype(BF)
+        actsqT[:, rows(i)] = actsT[:, rows(own_block(i, k))]
+
+    sdn.stage(1)
+    send_home(0, block)
+    attT = lambda t: att[:, t * 192:(t + 1) * 192]
+
+    def out_rows(t):
+        aT = att[:, t * 384:(t + 1) * 384].T.astype(BF)
+        g = nn(aT, agrad[...]).astype(BF)
+        GO[2 * t:2 * t + 2] = g.reshape(2, 2, 2, 48, 768)
+    for t in range(2): out_rows(t)
+    sup.stage(1)
+    sout.stage(0)
+    dK[...] = jnp.zeros_like(dK)
+    dV[...] = jnp.zeros_like(dV)
+    ck.wait(); cv.wait()
+
+    def heads(h):
+        lanes = rows(h)
+        KT[...] = K[:, lanes].T
+        at = 0
+        for i in range(4):
+            kk = 256 * (i + 1)
+            r = slice(i * 128, (i + 1) * 128)
+            d = da[r, lanes]
+            qb, db = spread(Q[r, lanes]), spread(d)
+            prod = (d.astype(F32) * att[r, lanes]).T
+            delta = jnp.concatenate([jnp.sum(prod[:64], axis=0, keepdims=True), jnp.sum(prod[64:], axis=0, keepdims=True)], axis=1)
+            st = nt(K[0:kk, lanes], qb) + bias[at:at + kk, :]
+            p = jnp.exp(st - lse[h, i:i + 1, :])
+            ds = (p * (nt(V[0:kk, lanes], db) - delta)).astype(BF)
+            dV[0:kk, lanes] += nn(p.astype(BF), db)
+            dK[0:kk, lanes] += nn(ds, qb)
+            dQ[r, lanes] = pick(nn(KT[:, 0:kk], ds)) * 0.125
+            at += kk
+
+    pl.loop(0, 1)(heads)
+    sdn.stage(2)
+    pl.loop(1, 2)(heads)
+    sout.stage(1)
+    home_across(0)
+    pl.loop(2, 3)(heads)
+    sdn.stage(3)
+    sup.stage(2)
+    pl.loop(3, 4)(heads)
+    sout.stage(2)
+    pl.loop(4, 5)(heads)
+    sdn.stage(4)
+    sup.stage(3)
+    sout.stage(3)
+    pl.loop(5, 6)(heads)
+    V[...] = dV[...].astype(BF)
+    put_vec(24, jnp.sum(V[...].astype(F32), axis=0, keepdims=True))
+
+    def weight_rows(n, lhs, g):
+        @pl.loop(0, 4)
+        def _(t):
+            GQ[n, t] = nn(lhs[rows(t, 192), :], g[...]).astype(BF).reshape(2, 2, 48, 768)
+    weight_rows(2, actsT, V)
+    sv.stage(0)
+
+    @pl.loop(0, 8)
+    def _(j):
+        c, s = table_rows(COS, SIN, length, j)
+        for t in range(6):
+            u = dK[rows(j), t * 128:(t + 1) * 128]
+            K[rows(j), t * 128:(t + 1) * 128] = (u * c - swap(u) * s).astype(BF)
+        dK[rows(j), :] = nt(K[rows(j), :], matrix(WQ, slice(768, 1536))) + nt(V[rows(j), :], matrix(WQ, slice(1536, 2304)))
+
+    @pl.loop(0, 4)
+    def _(i):
+        j = own_block(i, k)
+        c, s = table_rows(COS, SIN, length, j)
+        for t in range(6):
+            u = dQ[rows(i), t * 128:(t + 1) * 128]
+            da[rows(i), t * 128:(t + 1) * 128] = (u * c - swap(u) * s).astype(BF)
+        dK[rows(j), :] += nt(da[rows(i), :], matrix(WQ, slice(0, 768)))
+        es[i] = dK[rows(own_block(i, 1 - k)), :].astype(BF)
+
+    ecp = remote(es, er, esem_s, esem_r, sib)
+    ecp.start()
+    put_vec(18, jnp.sum(K[...].astype(F32), axis=0, keepdims=True))
+    put_vec(12, jnp.sum(da[...].astype(F32), axis=0, keepdims=True))
+    sv.stage(1)
+    weight_rows(1, actsT, K)
+    sk.stage(0)
+    ecp.wait_recv()
+    gg = jnp.zeros((1, 768), F32)
+    gsh = jnp.zeros((1, 768), F32)
     for i in range(4):
-        bl[i] = block[i * 128:(i + 1) * 128, :].astype(BF)
-    send_home(0, bl)
-
-    def token_grads():
-        ecp.wait_recv()
-        gg = jnp.zeros((1, 768), F32)
-        gsh = jnp.zeros((1, 768), F32)
-        for i in range(4):
-            j = own_block(jnp.int32(i), k)
-            n, inv = norm(X[j].astype(F32))
-            ee = e[rows(j), :] + er[i].astype(F32)
-            gg += jnp.sum(ee * n, axis=0, keepdims=True)
-            gsh += jnp.sum(ee, axis=0, keepdims=True)
-            gx[i] = (gmid[i * 128:(i + 1) * 128, :] + norm_grad(ee, n, inv, gain[...])).astype(BF)
-        send_home(1, gx)
-        vbuf[0] = vin[...]
-        for t in range(6):
-            vbuf[0, t:t + 1, :] = gg[:, t * 128:(t + 1) * 128]
-            vbuf[0, 6 + t:7 + t, :] = gsh[:, t * 128:(t + 1) * 128]
-
-    sc = gs[0]
-    vec_steps = [[sib], [dev(z, *sc.p2, k)], [dev(z, *sc.p3, k)], [dev(lax.rem(z + d, 4), y, x, k) for d in (1, 2, 3)]]
+        n, inv = norm(X[i].astype(F32))
+        ee = dK[rows(own_block(jnp.int32(i), k)), :] + er[i].astype(F32)
+        gg += jnp.sum(ee * n, axis=0, keepdims=True)
+        gsh += jnp.sum(ee, axis=0, keepdims=True)
+        gx[i] = (gmid[i * 128:(i + 1) * 128, :] + norm_grad(ee, n, inv, gain[0:1, :])).astype(BF)
+    send_home(1, gx)
+    put_vec(0, gg); put_vec(6, gsh)
+
+    vec_steps = [[sib], [dev(z, *sq.p2, k)], [dev(z, *sq.p3, k)], [dev(lax.rem(z + d, 4), y, x, k) for d in (1, 2, 3)]]
     vcp = []
     def vec_stage(n):
         if n > 0:
@@ -1535,57 +1653,62 @@
             vcp.append([remote(vbuf.at[n], vrec.at[n + i], vsend.at[n + i], vrecv.at[n + i], d) for i, d in enumerate(vec_steps[n])])
             for c in vcp[-1]: c.start()
 
-    for tick in range(len(gs) + Scatter.STAGES - 1):
-        for i, gg_ in enumerate(gs):
-            n = tick - i
-            if 0 <= n < Scatter.STAGES:
-                gg_.stage(n)
-        if tick == 0:
-            token_grads()
-        if 1 <= tick <= 5:
-            vec_stage(tick - 1)
-    lst = remote(fin.at[1 - k], fsib, misc_s.at[1], misc_r.at[1], sib)
-    lst.start()
-    lst.wait_recv()
-    for i, o in enumerate((oq, oo, ou)):
-        mine = fin[k, :, offs[i]:offs[i] + halves[i]]
-        theirs = fsib[:, offs[i]:offs[i] + halves[i]]
-        o[:, :halves[i]] = jnp.where(k == 0, mine, theirs)
-        o[:, halves[i]:] = jnp.where(k == 0, theirs, mine)
-    for a in range(2):
-        for i in range(2):
-            remote(H0.at[a, i], H0.at[a, i], hsend.at[0, 0, 0], h0.at[a, i], sib).wait_recv()
-            remote(HL.at[a, i], HL.at[a, i], hsend.at[0, 0, 0], hl.at[a, i], sib).wait_recv()
-            remote(HS.at[a, i], HS.at[a, i], hsend.at[0, 0, 0], hs.at[a, i], sib).wait_recv()
-    lst.wait_send()
+    vec_stage(0)
+    weight_rows(0, actsqT, da)
+    sq.stage(0)
+    sk.stage(1)
+    sv.stage(2)
+    sq.stage(1)
+    sup.stage(4)
+    sout.stage(4)
+    vec_stage(1)
+    home_across(1)
+    sk.stage(2)
+    sv.stage(3)
+    sq.stage(2)
+    vec_stage(2)
+    sdn.stage(5); sout.stage(5); sup.stage(5)
+    sk.stage(3)
+    sq.stage(3)
+    vec_stage(3)
+    sv.stage(4)
+    sk.stage(4)
+    sq.stage(4)
+    vec_stage(4)
+    home_done(0)
+    sv.stage(5); sk.stage(5); sq.stage(5)
+    home_done(1)
     ecp.wait_send()
     for cs in vcp:
         for c in cs: c.wait_send()
+    for c in across: c.wait_send()
     for cp, cond in homes:
         @pl.when(cond)
         def _():
             cp.wait_send()
 
 
-def reduce_call(flag, gqkv, gout, gup, gdown, *ins):
-    cols = (gqkv.shape[1], gout.shape[1], gup.shape[1])
-    gqkv, gout, gup = (g.reshape(4, 2, 2, 48, g.shape[1]) for g in (gqkv, gout, gup))
+def backward_call(gup, gdown, block, *ins):
+    n_up = gup.shape[1]
+    gup = gup.reshape(4, 2, 2, 48, n_up)
     gdown = gdown.reshape(4, 2, 2, 2, 96, 768)
     any_ = pl.BlockSpec(memory_space=pl.ANY)
-    bufs = []
-    for r, n in ((48, cols[0] // 2), (48, cols[1] // 2), (48, cols[2] // 2), (96, 768)):
-        bufs += [VM((4, 2, 2, r, n), BF), VM((4, 2, 2, r, n), BF), VM((2, 4, r, n), BF), VM((4, r, n), BF), VM((3, r, n), BF)]
-    H = sum(cols) // 2
+    def bufs(r, n, lead=()):
+        return [VM(lead + s + (r, n), BF) for s in ((4, 2, 2), (2, 4), (4,), (3,))]
     DS = pltpu.SemaphoreType.DMA
     home = sd((2, 2, 128, 768), BF)
-    return pl.pallas_call(functools.partial(reduce_kernel, cols),
-        out_shape=[sd((24, cols[0]), F32), sd((24, cols[1]), F32), sd((24, cols[2]), F32), sd((96, 768), F32), sd((80, 128), F32), home, home, home],
-        in_specs=[ss] + [vs] * (4 + len(ins)), out_specs=[vs] * 5 + [any_] * 3,
-        scratch_shapes=bufs + [VM((2, 24, H), F32), VM((24, H), F32), VM((4, 128, 768), BF), VM((4, 128, 768), BF), VM((4, 128, 768), BF),
-                               VM((4, 128, 768), BF), VM((4, 80, 128), F32), VM((6, 80, 128), F32),
-                               DS((4, 7)), DS((4, 7)), DS((2, 4, 3)), DS((2, 2)), DS((2, 2)), DS((2, 2)), DS((2,)), DS((2,)), DS((6,)), DS((6,))],
-        compiler_params=pltpu.CompilerParams(collective_id=1, has_side_effects=True, vmem_limit_bytes=62 * 2**20),
-    )(flag, gqkv, gout, gup, gdown, *ins)
+    return pl.pallas_call(backward_kernel,
+        out_shape=[sd((24, 2304), F32), sd((24, 768), F32), sd((24, 3072), F32), sd((96, 768), F32), sd((80, 128), F32), home, home, home],
+        in_specs=[any_] * 3 + [vs] * 4 + [any_] * 2 + [vs] * 8, out_specs=[vs] * 5 + [any_] * 3,
+        scratch_shapes=[VM((1024, 768), BF), VM((1024, 768), BF), VM((2560, 256), F32), VM((128, 1024), BF), VM((512, 768), BF), VM((512, 768), F32),
+                        VM((1024, 768), F32), VM((1024, 768), F32), VM((512, 768), BF), VM((768, 512), BF),
+                        VM((4, 2, 2, 48, 768), BF), VM((3, 4, 2, 2, 48, 768), BF), VM((4, 2, 2, 48, 1536), BF), VM((4, 2, 2, 96, 768), BF)]
+        + bufs(48, 1536) + bufs(96, 768) + bufs(48, 384) + bufs(48, 384, (3,))
+        + [VM((4, 2, 24, 384), F32), VM((4, 24, 384), F32), VM((1, 2, 24, 1536), F32), VM((1, 24, 1536), F32),
+           VM((4, 128, 768), BF), VM((4, 128, 768), BF), VM((4, 128, 768), BF), VM((4, 80, 128), F32), VM((6, 80, 128), F32),
+           DS((6, 7)), DS((6, 7)), DS((2,)), DS((6,)), DS((6,)), DS((2, 4, 2)), DS((2, 2)), DS((2, 2)), DS((2, 2)), DS((2, 2)), DS, DS, DS((6,)), DS((6,)), DS((2,))],
+        compiler_params=pltpu.CompilerParams(collective_id=1, has_side_effects=True, vmem_limit_bytes=63 * 2**20),
+    )(gup, gdown, block, *ins)
 
 def fast_shards(inputs, history, seq_lengths, attn_gain, attn_shift, qkv_weight, qkv_bias, out_weight, out_bias, mlp_gain,
                 mlp_shift, up_weight, up_bias, down_weight, down_bias, mix_weights, cotangent):
@@ -1596,16 +1719,13 @@
     packed = jnp.stack([jnp.pad(v.astype(F32), (0, 128 - v.shape[0])) for v in vectors])
     packed = packed.at[0, 64:66].set(lens)
     COS, SIN = (jnp.asarray(t) for t in rope_tables())
-    X, acts, Q, K, V, att, lse, WQ, WO, block, gmid, gup, gdown, gain, vgrad = forward_call(
+    X, actsT, Q, K, V, att, lse, WQ, WO, block, gmid, gup, gdown, gain, vgrad = forward_call(
         qkv_weight, out_weight, up_weight, down_weight, packed, inputs, cotangent, COS, SIN, mix_weights)
-    wqkv, wout, a_gain = WQ.reshape(768, 2304), WO.reshape(768, 768), gain[:1]
-    flag = (vgrad[79, :1] == LONG_LEN).astype(jnp.int32)
-    e, gqkv, gout, g_bqkv, g_bout = attn_bwd_call(flag, gmid, acts, Q, K, V, att, lse, wqkv, wout, COS, SIN)
     earlier, cot = history.astype(F32), cotangent.astype(F32)
     mix_terms = jnp.sum(earlier * cot[None], axis=(1, 2, 3))
     grad_history = (mix_weights[:-1, None, None, None] * cot[None]).astype(BF)
-    vin = vgrad.at[12:30].set(g_bqkv.reshape(18, 128)).at[30:36].set(g_bout.reshape(6, 128)).at[78, :5].set(mix_terms)
-    oq, oo, ou, od, vout, H0, HL, HS = reduce_call(flag, gqkv, gout, gup, gdown, e, gmid, block, X, a_gain, vin)
+    vin = vgrad.at[78, :5].set(mix_terms)
+    oq, oo, ou, od, vout, H0, HL, HS = backward_call(gup, gdown, block, gmid, X, actsT, Q, K, V, att, lse, WQ, WO, gain, COS, SIN, vin)
     is_long = (seq_lengths == LONG_LEN)[None, :, None, None]
     other = jnp.where(is_long, HL, HS)
     home = jnp.where(y == 0, jnp.concatenate([H0, other], axis=2), jnp.concatenate([other, H0], axis=2))

time: 326 us -> 289 us (0.89); the launches traced: 325 us -> 284 us
  Pallas kernels: 285 us -> 251 us
  local copies, waits for them, and re-layouts: 21.4 us -> 17 us
    pallas_call x2 -> x1, Pallas kernels: 152 us -> 117 us  [backward_call(): pl.pallas_call(backward_kernel, out_shape=[sd((24, 2304), F32), sd((24, 7...]
where the time goes in v3:
time: 289 us; the launch traced here: 284 us
  Pallas kernels  251 us (87%)
  local copies, waits for them, and re-layouts  17 us (6%)
  other arithmetic  14.9 us (5%)
    pallas_call x1, Pallas kernels, forward_call(): pl.pallas_call(functools.partial(forward_kernel, cols), out_shape=[sd(*t)...  134 us
    pallas_call x1, Pallas kernels, backward_call(): pl.pallas_call(backward_kernel, out_shape=[sd((24, 2304), F32), sd((24, 7...  117 us
    reduce_sum x1, other arithmetic, fast_shards(): mix_terms = jnp.sum(earlier * cot[None], axis=(1, 2, 3))  6.83 us

profile of v3, /device:TPU:0, one launch (start us, length us, event | category | flops | bytes accessed | tf_op | source)
XLA Modules:
  0.0 284.1 jit_solution(11470142588071723153)
XLA Ops:
  0.6 0.0 copy-start.1
  0.7 0.7 pad_bitcast_fusion.2
  1.4 0.7 pad_bitcast_fusion.4
  2.1 0.7 pad_bitcast_fusion.6
  2.8 0.7 pad_bitcast_fusion
  3.5 0.6 fusion.4
  4.1 1.3 and_reduce_fusion
  5.4 2.7 broadcast_select_fusion.1
  8.0 1.6 scatter.6.vec
  9.6 0.6 copy-done.7
  10.2 133.7 %shard_map.306 = (bf16[4,128,768]{2,1,0:T(8,128)(2,1)}, bf16[768,1024]{1,0:T(8,128)(2,1)}, bf16[512,768]{1,0:T(8,128)(2,1)}, bf16[1024,768]{1,0:T(8,128)(2,1)}, ...) custom-call(bf16[24,2304]{1,0:T(8,128)(2,1)} %qkv.1, ...), custom_call_target="tpu_custom_call" | custom-call | tf_op jit(solution)/shard_map/pallas_call | solution.py:1373
  143.9 0.0 copy-start.8
  144.0 0.1 convert_element_type.40
  144.1 0.5 copy-done.8
  144.6 6.8 %fusion.1 = (f32[5]{0:T(128)S(1)}, f32[2,256,768]{2,1,0:T(8,128)}, bf16[5,2,256,768]{3,2,1,0:T(8,128)(2,1)}) fusion(bf16[5,2,256,768]{3,2,1,0:T(8,128)(2,1)} %param.24, f32[2,256,768]{2,1,0:T(8,128)S(1)} %convert_element_type.40, f32[5]{0:T(128)S(1)} %bitcast.34), kind=kLoop, calls=%fused_computation.3 | loop fusion | flops 13369339 | bytes 11010088 | tf_op jit(solution)/shard_map/reduce_sum | solution.py:1725
  151.4 1.3 scatter.9.vin
  152.7 117.3 %shard_map.307 = (f32[24,2304]{1,0:T(8,128)}, f32[24,768]{1,0:T(8,128)}, f32[24,3072]{1,0:T(8,128)}, f32[96,768]{1,0:T(8,128)}, f32[80,128]{1,0:T(8,128)}, /*ind...) custom-call(bf16[4,2,2,48,3072]{4,3,2,1,0:T(8,128)(2,1)} %bitcast.32, ...), custom_call_target="tpu_custom_call" | custom-call | tf_op jit(solution)/shard_map/pallas_call | solution.py:1700
  270.0 0.0 copy-start.2
  270.1 1.6 broadcast_select_fusion
  271.7 0.6 maximum_select_fusion
  272.3 0.6 slice.58
  272.9 0.2 copy-done
  273.1 1.7 fusion.2
  274.8 0.9 slice_bitcast_fusion
  275.7 1.4 fusion.3
  277.1 1.3 dynamic_slice.26
  278.4 1.3 dynamic_slice.30
  279.7 1.2 slice.66
  280.9 0.7 copy.41
  281.6 0.6 copy.42
  282.2 0.7 copy.43
  282.9 0.7 copy.44
  (18 shorter events, 0.1 us)
Async XLA Ops:
  0.6 143.3 %copy-start.1 = (bf16[2,256,768]{2,1,0:T(8,128)(2,1)S(1)}, bf16[2,256,768]{2,1,0:T(8,128)(2,1)}, u32[]{:S(2)}) copy-start(bf16[2,256,768]{2,1,0:T(8,128)(2,1)} %cin.1) | copy-start | bytes 2359300
  9.6 0.6 copy-start.7
  143.9 0.7 copy-start.8
  152.7 117.3 %copy-start.9 = (s32[2]{0:T(128)S(1)}, s32[2]{0:T(128)}, u32[]{:S(2)}) copy-start(s32[2]{0:T(128)} %param.25) | copy-start | bytes 28
  270.0 1.6 copy-start.2
  271.7 1.4 copy-start
  274.8 6.1 %copy-start.5 = (f32[24,2304]{1,0:T(8,128)S(1)}, f32[24,2304]{1,0:T(8,128)}, u32[]{:S(2)}) copy-start(f32[24,2304]{1,0:T(8,128)} %get-tuple-element.126) | copy-start | bytes 663556
  274.8 6.8 %copy-start.6 = (f32[24,768]{1,0:T(8,128)S(1)}, f32[24,768]{1,0:T(8,128)}, u32[]{:S(2)}) copy-start(f32[24,768]{1,0:T(8,128)} %get-tuple-element.128) | copy-start | bytes 221188
  274.8 7.4 %copy-start.4 = (f32[24,3072]{1,0:T(8,128)S(1)}, f32[24,3072]{1,0:T(8,128)}, u32[]{:S(2)}) copy-start(f32[24,3072]{1,0:T(8,128)} %get-tuple-element.132) | copy-start | bytes 884740
  274.8 8.1 %copy-start.3 = (f32[96,768]{1,0:T(8,128)S(1)}, f32[96,768]{1,0:T(8,128)}, u32[]{:S(2)}) copy-start(f32[96,768]{1,0:T(8,128)} %get-tuple-element.134) | copy-start | bytes 884740
